TPU v7x, 512 devices: a whole 4x4x16 slice. The times are simulated.
512 devices in a mesh: dp: 128 (over y, z, core), rep: 4 (over x).
Axes of the slice: x: 4, y: 4, z: 16, core: 2. Of those that a mesh axis runs over, the one named last changes fastest.
Arguments:
- q_raw: bfloat16 [3, 1536, 8192], P(None, 'dp', 'rep'), may hold values from -16 to 16
- k_raw: bfloat16 [3, 1536, 512], P(None, 'dp', 'rep'), may hold values from -8 to 8
- v_raw: bfloat16 [3, 1536, 512], P(None, 'dp', 'rep'), may hold values from -6 to 6
- q_gain: float32 [128], replicated, may hold values from 0.6 to 5.5
- k_gain: float32 [128], replicated, may hold values from 0.6 to 5.5
- kv_pool: bfloat16 [6144, 64, 2, 512], P('dp', None, None, 'rep'), may hold values from -6 to 6
- page_table: int32 [1536, 4], P('dp'), may hold values from 0 to 47, as said below
- cache_len: int32 [1536], P('dp'), may hold values from 1 to 253, as said below
- out_pages: int32 [1024], P('dp'), may hold values from 0 to 47, as said below
- in_slots: int32 [1024], P('dp'), may hold values from 0 to 47, as said below
- hidden_in: bfloat16 [3, 1536, 4096], P(None, 'dp', 'rep'), may hold values from -48 to 48
- ln_gain: float32 [4096], replicated, may hold values from 0.1 to 1.9
- route_ids: int32 [3, 1536, 8], P(None, 'dp'), may hold values from 0 to 63, all different within a row; in each aligned block of 12 rows (0 to 11, 12 to 23, ..., all dimensions but the last counted through in order) at most 2 rows name the same one
- route_logits: float32 [3, 1536, 8], P(None, 'dp'), may hold values from -4 to 4
- w_gate: bfloat16 [128, 4096, 512], P('dp', None, 'rep'), may hold values from -0.09375 to 0.09375
- w_up: bfloat16 [128, 4096, 512], P('dp', None, 'rep'), may hold values from -0.09375 to 0.09375
- w_down: bfloat16 [128, 512, 4096], P('dp', None, 'rep'), may hold values from -0.1875 to 0.1875
Outputs:
- attn_out: bfloat16 [3, 1536, 8192], P(None, 'dp', 'rep')
- moe_out: bfloat16 [3, 1536, 4096], P(None, 'dp', 'rep')
Inputs may be any that keep to these rules, and one draw needn't show every extreme that they name: `route_ids`: each row names 8 different experts; in each step the 12 rows of one dp index name no expert more than 2 times, a bound that some block reaches. `page_table`: the 12 rows of one dp index hold each page number of that index once. `cache_len`: the first request holds the most. `out_pages`: the 8 entries of one dp index are different pages. `in_slots`: the 8 entries of one dp index are different pages.
All inputs are finite; a program needn't handle non-finite values.
Results may differ from a plain program's by a relative error of at most 0.008.
Values may be sent and summed in bfloat16 or wider, within the bound.
A program may use at most 64 MiB of HBM per device.

v0:
```python
import math

import jax
import jax.numpy as jnp
from jax import lax
from jax.sharding import PartitionSpec as P

D = 4096
HEAD_DIM = 128
EXPERTS = 64
STEPS = 3
CAPACITY = 2


EPS = 1e-06
THETA = 1000000.0


def from_behind(x, axis, by):
    size = lax.axis_size(axis)
    return lax.ppermute(x, axis, [(i, (i + by) % size) for i in range(size)])


def head_norm(values, gain):
    mean_square = jnp.mean(values * values, axis=-1, keepdims=True)
    return values * lax.rsqrt(mean_square + EPS) * gain


def rotate(values, position):
    half_dim = values.shape[-1] // 2
    exponent = jnp.arange(half_dim, dtype=jnp.float32) * (2.0 / values.shape[-1])
    frequency = THETA ** (-exponent)
    angle = position.astype(jnp.float32)[:, None] * frequency[None, :]
    cosine = jnp.cos(angle)[:, None, :]
    sine_part = jnp.sin(angle)[:, None, :]
    first_half = values[..., :half_dim]
    second_half = values[..., half_dim:]
    return jnp.concatenate(
        [
            first_half * cosine - second_half * sine_part,
            second_half * cosine + first_half * sine_part,
        ],
        axis=-1,
    )


def attend(context, lengths, queries_in, keys_in, values_in, q_gain, k_gain):
    row_count, span_len, _, kv_width = context.shape
    kv_count = kv_width // HEAD_DIM
    q_count = queries_in.shape[-1] // HEAD_DIM
    groups = q_count // kv_count
    places = jnp.arange(span_len, dtype=jnp.int32)
    scaling = 1.0 / math.sqrt(HEAD_DIM)
    results = []
    for step_index in range(STEPS):
        position = lengths + step_index
        queries = queries_in[step_index].astype(jnp.float32).reshape(row_count, q_count, HEAD_DIM)
        queries = rotate(head_norm(queries, q_gain), position).astype(jnp.bfloat16)
        new_keys = keys_in[step_index].astype(jnp.float32).reshape(row_count, kv_count, HEAD_DIM)
        new_keys = rotate(head_norm(new_keys, k_gain), position).astype(jnp.bfloat16)
        fresh_rows = jnp.stack(
            [new_keys.reshape(row_count, kv_width), values_in[step_index]], axis=1
        )
        landing = (places[None, :] == position[:, None])[:, :, None, None]
        context = jnp.where(landing, fresh_rows[:, None, :, :], context)
        key_rows = context[:, :, 0, :].reshape(row_count, span_len, kv_count, HEAD_DIM)
        value_rows = context[:, :, 1, :].reshape(row_count, span_len, kv_count, HEAD_DIM)
        grouped = queries.reshape(row_count, kv_count, groups, HEAD_DIM)
        scores = (
            jnp.einsum("rhgd,rshd->rhgs", grouped, key_rows, preferred_element_type=jnp.float32)
            * scaling
        )
        valid = (places[None, :] <= position[:, None])[:, None, None, :]
        scores = jnp.where(valid, scores, -1e30)
        row_top = jnp.max(scores, axis=-1, keepdims=True)
        expos = jnp.where(valid, jnp.exp(scores - row_top), 0.0)
        probs = (expos / jnp.sum(expos, axis=-1, keepdims=True)).astype(jnp.bfloat16)
        mixed = jnp.einsum("rhgs,rshd->rhgd", probs, value_rows, preferred_element_type=jnp.float32)
        results.append(mixed.reshape(row_count, q_count * HEAD_DIM).astype(jnp.bfloat16))
    return jnp.stack(results)


def place(route_ids):
    flat_ids = route_ids.reshape(route_ids.shape[0], -1)
    hot_table = (
        flat_ids[:, :, None] == jnp.arange(EXPERTS, dtype=jnp.int32)[None, None, :]
    ).astype(jnp.int32)
    before = jnp.cumsum(hot_table, axis=1) - hot_table
    return jnp.sum(before * hot_table, axis=2).reshape(route_ids.shape)


def local(
    q_raw,
    k_raw,
    v_raw,
    q_gain,
    k_gain,
    kv_pool,
    page_table,
    cache_len,
    out_pages,
    in_slots,
    hidden_in,
    ln_gain,
    route_ids,
    route_logits,
    w_gate,
    w_up,
    w_down,
):
    ranks = lax.axis_size("dp")
    leaving = kv_pool[out_pages]
    arriving = from_behind(leaving, "dp", ranks // 2)
    pool = kv_pool.at[in_slots].set(arriving)
    context = pool[page_table]
    row_count, page_count, page_len, kv_pair, kv_width = context.shape
    context = context.reshape(row_count, page_count * page_len, kv_pair, kv_width)
    attn_out = attend(context, cache_len, q_raw, k_raw, v_raw, q_gain, k_gain)
    whole_rows = lax.all_gather(hidden_in, "rep", axis=2, tiled=True)
    values = whole_rows.astype(jnp.float32)
    mean_square = jnp.mean(values * values, axis=-1, keepdims=True)
    normed = (values * lax.rsqrt(mean_square + EPS) * ln_gain).astype(jnp.bfloat16)
    slots = place(route_ids)
    targets = route_ids * CAPACITY + slots
    expert_slots = jnp.arange(EXPERTS * CAPACITY, dtype=jnp.int32)
    hits = jnp.any(targets[:, None, :, :] == expert_slots[None, :, None, None], axis=-1)
    hits = hits.astype(jnp.bfloat16).reshape(STEPS, EXPERTS, CAPACITY, row_count)
    packed = jnp.einsum("secr,srd->escd", hits, normed, preferred_element_type=jnp.float32).astype(
        jnp.bfloat16
    )
    outgoing = jnp.broadcast_to(packed[None], (2,) + packed.shape).reshape(
        ranks, -1, packed.shape[-1]
    )
    incoming = lax.all_to_all(outgoing, "dp", split_axis=0, concat_axis=0, tiled=True)
    local_count = w_gate.shape[0]
    arrived = incoming.reshape(ranks, local_count, STEPS * CAPACITY, D)
    gate = jnp.einsum("nlrd,ldf->nlrf", arrived, w_gate, preferred_element_type=jnp.float32)
    upper = jnp.einsum("nlrd,ldf->nlrf", arrived, w_up, preferred_element_type=jnp.float32)
    hidden_part = (jax.nn.silu(gate) * upper).astype(jnp.bfloat16)
    hidden_all = lax.all_gather(hidden_part, "rep", axis=3, tiled=True)
    produced = jnp.einsum(
        "nlrf,lfd->nlrd", hidden_all, w_down, preferred_element_type=jnp.float32
    ).astype(jnp.bfloat16)
    returned = lax.all_to_all(
        produced.reshape(ranks, -1, produced.shape[-1]),
        "dp",
        split_axis=0,
        concat_axis=0,
        tiled=True,
    )
    returned = returned.reshape(2, EXPERTS, STEPS, CAPACITY, -1).astype(jnp.float32)
    both_halves = returned[0] + returned[1]
    section_index = jnp.broadcast_to(
        jnp.arange(STEPS, dtype=jnp.int32)[:, None, None], route_ids.shape
    )
    picked = both_halves[route_ids, section_index, slots]
    weights = jax.nn.softmax(route_logits, axis=-1)
    moe_out = jnp.sum(weights[..., None] * picked, axis=2).astype(jnp.bfloat16)
    return (attn_out, moe_out)


def solution(mesh):
    return jax.shard_map(
        local,
        mesh=mesh,
        in_specs=(
            P(None, "dp", "rep"),
            P(None, "dp", "rep"),
            P(None, "dp", "rep"),
            P(),
            P(),
            P("dp", None, None, "rep"),
            P("dp", None),
            P("dp"),
            P("dp"),
            P("dp"),
            P(None, "dp", "rep"),
            P(),
            P(None, "dp", None),
            P(None, "dp", None),
            P("dp", None, "rep"),
            P("dp", None, "rep"),
            P("dp", None, "rep"),
        ),
        out_specs=(P(None, "dp", "rep"), P(None, "dp", "rep")),
        check_vma=False,
    )
```

profile of v0, /device:TPU:1, one launch (start us, length us, event | category | flops | bytes accessed | tf_op | source)
XLA Modules:
  0.0 592.0 jit_solution(6714871857765084571)
XLA Ops:
  0.7 1.5 copy.99
  3.3 10.8 %all_gather.6 = bf16[3,12,4096]{2,1,0:T(8,128)(2,1)S(1)} all-gather(bf16[3,12,1024]{2,1,0:T(8,128)(2,1)S(1)} %copy-done.4), channel_id=1, replica_groups=mesh['dp'=128,'rep'=4] {'rep'}, dimensions={2}, use_global_device_ids=true | all-gather | bytes 368640 | tf_op jit(solution)/shard_map/all_gather | solution.py:119
  16.1 6.7 %copy.69 = bf16[128,6,4096]{2,1,0:T(8,128)(2,1)} copy(bf16[128,6,4096]{2,0,1:T(8,128)(2,1)S(1)} %bitcast.109) | data formatting | bytes 12582912 | tf_op jit(solution)/shard_map/reshape | solution.py:131
  22.9 23.2 %all-to-all-start = ((bf16[128,6,4096]{2,1,0:T(8,128)(2,1)}), bf16[128,6,4096]{2,1,0:T(8,128)(2,1)}, u32[]{:S(2)}, u32[]{:S(2)}) async-start(bf16[128,6,4096]{2,1,0:T(8,128)(2,1)} %copy.69), calls=%async_computation | async-start | bytes 16777216 | tf_op jit(solution)/shard_map/all_to_all | solution.py:134
  47.2 5.4 collective-permute-start
  54.1 355.3 %all-to-all-done = bf16[128,6,4096]{2,1,0:T(8,128)(2,1)} async-done(((bf16[128,6,4096]{2,1,0:T(8,128)(2,1)}), bf16[128,6,4096]{2,1,0:T(8,128)(2,1)}, u32[]{:S(2)}, u32[]{:S(2)}) %all-to-all-start) | async-done | bytes 6291488 | tf_op jit(solution)/shard_map/all_to_all | solution.py:134
  409.3 10.4 %fusion.9 = f32[128,1,6,128]{3,0,2,1:T(8,128)S(1)} fusion(bf16[128,6,4096]{2,1,0:T(8,128)(2,1)} %all-to-all-done, bf16[1,4096,128]{2,1,0:T(8,128)(2,1)} %param.31), kind=kOutput, calls=%fused_computation.20 | convolution fusion | flops 805306368 | bytes 7733248 | tf_op jit(solution)/shard_map/nlrd,ldf->nlrf/dot_general | solution.py:137
  419.7 23.1 %fusion.21 = bf16[128,1,6,128]{3,0,2,1:T(8,128)(2,1)S(1)} fusion(bf16[128,6,4096]{2,1,0:T(8,128)(2,1)} %all-to-all-done, bf16[1,4096,128]{2,1,0:T(8,128)(2,1)S(1)} %copy-done.23, f32[128,1,6,128]{3,0,2,1:T(8,128)S(1)} %fusion.9), kind=kOutput, calls=%fused_computation.27 | convolution fusion | flops 805896192 | bytes 7929856 | tf_op jit(solution)/shard_map/nlrd,ldf->nlrf/dot_general | solution.py:138
  442.8 13.7 %all_gather.7 = bf16[128,1,6,512]{3,0,2,1:T(8,128)(2,1)S(1)} all-gather(bf16[128,1,6,128]{3,0,2,1:T(8,128)(2,1)S(1)} %fusion.21), channel_id=1, replica_groups=mesh['dp'=128,'rep'=4] {'rep'}, dimensions={3}, use_global_device_ids=true | all-gather | bytes 983040 | tf_op jit(solution)/shard_map/all_gather | solution.py:140
  457.5 2.2 copy.72
  459.6 18.5 %all-to-all-start.1 = ((bf16[128,6,1024]{2,1,0:T(8,128)(2,1)}), bf16[128,6,1024]{2,1,0:T(8,128)(2,1)}, u32[]{:S(2)}, u32[]{:S(2)}) async-start(bf16[128,6,1024]{2,1,0:T(8,128)(2,1)} %copy.72), calls=%async_computation.1 | async-start | bytes 4194304 | tf_op jit(solution)/shard_map/all_to_all | solution.py:144
  485.9 1.8 scatter_fusion
  487.7 6.6 %gather_fusion.1 = bf16[48,64,2,128]{3,2,1,0:T(2,128)(2,1)} fusion(bf16[48,64,2,128]{3,2,1,0:T(2,128)(2,1)S(1)} %scatter_fusion, s32[1024]{0:T(1024)S(1)} %pad_clamp_fusion), kind=kCustom, calls=%fused_computation.1 | custom fusion | bytes 3145920 | tf_op jit(solution)/shard_map/gather | solution.py:115
  494.4 1.8 copy.63
  496.3 3.6 broadcast_select_fusion
  499.9 1.2 copy-done.2
  501.7 1.5 convolution_convert_fusion.2
  503.3 1.6 fusion.25
  505.1 1.5 convolution_convert_fusion.3
  508.4 68.4 %all-to-all-done.1 = bf16[128,6,1024]{2,1,0:T(8,128)(2,1)} async-done(((bf16[128,6,1024]{2,1,0:T(8,128)(2,1)}), bf16[128,6,1024]{2,1,0:T(8,128)(2,1)}, u32[]{:S(2)}, u32[]{:S(2)}) %all-to-all-start.1) | async-done | bytes 1572896 | tf_op jit(solution)/shard_map/all_to_all | solution.py:144
  576.9 2.5 copy_convert_fusion
  579.8 1.2 copy.77
  581.0 8.5 %gather_fusion.2 = f32[288,1024]{1,0:T(8,128)} fusion(f32[64,3,2,1024]{3,2,1,0:T(2,128)S(1)} %copy.77, s32[288]{0:T(512)S(1)} %reshape.1023), kind=kCustom, calls=%fused_computation.2 | custom fusion | bytes 2362752 | tf_op jit(solution)/shard_map/gather | solution.py:156
  589.5 2.3 multiply_reduce_fusion
  (118 shorter events, 17.2 us)
Async XLA Ops:
  0.6 455.8 %copy-start = (bf16[1,512,1024]{2,1,0:T(8,128)(2,1)S(1)}, bf16[1,512,1024]{2,1,0:T(8,128)(2,1)}, u32[]{:S(2)}) copy-start(bf16[1,512,1024]{2,1,0:T(8,128)(2,1)} %param.33) | copy-start | bytes 3145732
  0.6 2.7 copy-start.4
  2.2 12.1 %copy-start.9 = (f32[4096]{0:T(1024)S(1)}, f32[4096]{0:T(1024)}, u32[]{:S(2)}) copy-start(f32[4096]{0:T(1024)} %param.28) | copy-start | bytes 49156
  22.9 23.2 %copy-start.24 = (s32[8]{0:T(128)S(1)}, s32[8]{0:T(128)}, u32[]{:S(2)}) copy-start(s32[8]{0:T(128)} %param.25) | copy-start | bytes 100
  22.9 29.8 %copy-start.19 = (s32[12,4]{0,1:T(4,128)S(1)}, s32[12,4]{0,1:T(4,128)}, u32[]{:S(2)}) copy-start(s32[12,4]{0,1:T(4,128)} %param.23) | copy-start | bytes 580
  22.9 30.6 %copy-start.3 = (bf16[3,12,2048]{2,1,0:T(8,128)(2,1)S(1)}, bf16[3,12,2048]{2,1,0:T(8,128)(2,1)}, u32[]{:S(2)}) copy-start(bf16[3,12,2048]{2,1,0:T(8,128)(2,1)} %param.17) | copy-start | bytes 442372
  22.9 386.4 %all-to-all-start = ((bf16[128,6,4096]{2,1,0:T(8,128)(2,1)}), bf16[128,6,4096]{2,1,0:T(8,128)(2,1)}, u32[]{:S(2)}, u32[]{:S(2)}) async-start(bf16[128,6,4096]{2,1,0:T(8,128)(2,1)} %copy.69), calls=%async_computation | async-start | bytes 16777216 | tf_op jit(solution)/shard_map/all_to_all | solution.py:134
  46.1 7.5 %copy-start.5 = (bf16[3,12,128]{2,1,0:T(8,128)(2,1)S(1)}, bf16[3,12,128]{2,1,0:T(8,128)(2,1)}, u32[]{:S(2)}) copy-start(bf16[3,12,128]{2,1,0:T(8,128)(2,1)} %param.18) | copy-start | bytes 27652
  46.1 7.7 %copy-start.20 = (s32[12]{0:T(128)S(1)}, s32[12]{0:T(128)}, u32[]{:S(2)}) copy-start(s32[12]{0:T(128)} %param.24) | copy-start | bytes 148
  46.1 7.7 %copy-start.21 = (f32[128]{0:T(128)S(1)}, f32[128]{0:T(128)}, u32[]{:S(2)}) copy-start(f32[128]{0:T(128)} %param.21) | copy-start | bytes 1540
  47.2 438.7 %collective-permute-start = (bf16[8,64,2,128]{3,2,1,0:T(2,128)(2,1)S(1)}, bf16[8,64,2,128]{3,2,1,0:T(2,128)(2,1)}, u32[]{:S(2)}, u32[]{:S(2)}) collective-permute-start(bf16[8,64,2,128]{3,2,1,0:T(2,128)(2,1)S(1)} %gather_fusion), channel_id=1, source_target_pairs={{0,256},{4,260},{8,264},{12,268},{16,272},{20,276},{24,280},{28,28... | collective-permute-start | bytes 786440 | tf_op jit(solution)/shard_map/ppermute | solution.py:21
  409.3 10.4 %copy-start.23 = (bf16[1,4096,128]{2,1,0:T(8,128)(2,1)S(1)}, bf16[1,4096,128]{2,1,0:T(8,128)(2,1)}, u32[]{:S(2)}) copy-start(bf16[1,4096,128]{2,1,0:T(8,128)(2,1)} %param.32) | copy-start | bytes 3145732
  459.6 18.5 %copy-start.15 = (bf16[3,12,128]{2,1,0:T(8,128)(2,1)S(1)}, bf16[3,12,128]{2,1,0:T(8,128)(2,1)}, u32[]{:S(2)}) copy-start(bf16[3,12,128]{2,1,0:T(8,128)(2,1)} %param.19) | copy-start | bytes 27652
  459.6 20.2 %copy-start.25 = (s32[8]{0:T(128)S(1)}, s32[8]{0:T(128)}, u32[]{:S(2)}) copy-start(s32[8]{0:T(128)} %param.26) | copy-start | bytes 100
  459.6 22.1 %copy-start.17 = (f32[3,12,8]{1,2,0:T(8,128)S(1)}, f32[3,12,8]{1,2,0:T(8,128)}, u32[]{:S(2)}) copy-start(f32[3,12,8]{1,2,0:T(8,128)} %param.30) | copy-start | bytes 3460
  459.6 117.2 %all-to-all-start.1 = ((bf16[128,6,1024]{2,1,0:T(8,128)(2,1)}), bf16[128,6,1024]{2,1,0:T(8,128)(2,1)}, u32[]{:S(2)}, u32[]{:S(2)}) async-start(bf16[128,6,1024]{2,1,0:T(8,128)(2,1)} %copy.72), calls=%async_computation.1 | async-start | bytes 4194304 | tf_op jit(solution)/shard_map/all_to_all | solution.py:144
  478.1 6.0 %copy-start.18 = (s32[48]{0:T(128)S(1)}, s32[48]{0:T(128)}, u32[]{:S(2)}) copy-start(s32[48]{0:T(128)} %reshape.1017) | copy-start | bytes 580
  483.2 2.7 copy-start.22
  494.3 1.9 copy-start.12
  494.3 1.9 copy-start.13
  494.4 1.9 copy-start.14
  496.3 4.8 copy-start.10
  503.3 3.4 copy-start.1
  503.3 3.4 copy-start.11
  (5 other events, 8.4 us)
where the time goes:
time: 593 us; the launch traced here: 592 us
  waiting for transfers between devices  424 us (72%)
  starting transfers between devices  47 us (8%)
  matrix products  41.2 us (7%)
  local copies, waits for them, and re-layouts  36 us (6%)
  blocking collectives  24.5 us (4%)
  other arithmetic  18.1 us (3%)
    all_to_all x1, waiting for transfers between devices, local(): lax.all_to_all(outgoing, 'dp', split_axis=0, concat_axis=0, tiled=True)  355 us
    all_to_all x1, waiting for transfers between devices, local(): lax.all_to_all(produced.reshape(ranks, -1, produced.shape[-1]), 'dp', spl...  68.4 us
    all_to_all x1, starting transfers between devices, local(): lax.all_to_all(outgoing, 'dp', split_axis=0, concat_axis=0, tiled=True)  23.2 us
    dot_general x1, matrix products, local(): jnp.einsum('nlrd,ldf->nlrf', arrived, w_up, preferred_element_type=jnp.fl...  23.1 us
    all_to_all x1, starting transfers between devices, local(): lax.all_to_all(produced.reshape(ranks, -1, produced.shape[-1]), 'dp', spl...  18.5 us
    all_gather x1, blocking collectives, local(): hidden_all = lax.all_gather(hidden_part, 'rep', axis=3, tiled=True)  13.7 us
  transfers between devices with their start and end apart: 3, of which 2 were waited for; matrix products, arithmetic and copies ran while one was open for 11% of the time, Pallas kernels for 0%

commit v1 on v0

v1 whole, which is shorter than its diff:
```python
import functools
import math

import jax
import jax.numpy as jnp
import numpy as np
from jax import lax
from jax.experimental import pallas as pl
from jax.experimental.pallas import tpu as pltpu
from jax.sharding import PartitionSpec as P

NX, NY, NZ, NC = 4, 4, 16, 2
STEPS, REQ, TOP_K = 3, 12, 8
D, HEAD_DIM = 4096, 128
EPS = 1e-06
THETA = 1000000.0

LB = 4
PACK = STEPS * LB * REQ
WIDE = D // NX // LB
GROUPS = NZ // 2
PER = 2
CHUNKS = GROUPS // PER
SLAB = LB * 2 * STEPS * 2
ROWS = SLAB // LB * NY * NC
CLASSES = 4
SEL = CLASSES * SLAB
HIDE = 128
MESH = pl.DeviceIdType.MESH
F32, BF16 = jnp.float32, jnp.bfloat16


def tables():
    spread = np.zeros((SEL, 64), np.float32)
    base = np.zeros((SEL, 128), np.float32)
    row = 0
    for cls in range(CLASSES):
        for lb in range(LB):
            for zz in range(2):
                for s in range(STEPS):
                    for slot in range(2):
                        spread[row, zz * 32 + cls * 6 + s * 2 + slot] = 1
                        base[row] = zz * PACK + s * LB * REQ + lb * REQ
                        row += 1
    peers, per = NY * NC, SLAB // LB
    perm = np.zeros((peers * SLAB, peers * SLAB), np.float32)
    for lb in range(LB):
        for q in range(peers):
            for r in range(per):
                perm[(lb * peers + q) * per + r, q * SLAB + lb * per + r] = 1
    token = np.zeros((PACK, 128), np.float32)
    for s in range(STEPS):
        for lb in range(LB):
            for i in range(REQ):
                token[(s * LB + lb) * REQ + i, s * REQ + i] = 1
    return spread, base, perm, token


def dot(a, b):
    return jnp.dot(a, b, preferred_element_type=F32)


def kernel(
    source_page, out_pages, lengths,
    scaled, squares, meta, pool, queries, fresh, cosines, sines, q_gain, k_gain,
    spread, base, perm, perm_back, token,
    w_gate, w_up, w_down,
    attn, moe,
    leave, arrive, stat, rows, metas, chosen, taken, w_in, w_out,
    part_own, part_out, part_in, hidden, back_out, back_in, total, ring_out, ring_in,
    local_sem, page_sem, stat_sem, w_sem, row_sem, meta_sem, taken_sem,
    part_sem, hidden_sem, back_sem, ring_sem,
):
    dp, x = lax.axis_index("dp"), lax.axis_index("rep")
    y, z, c = dp // (NZ * NC), (dp // NC) % NZ, dp % NC
    q = y * NC + c
    right = ((y * NZ + (z + 1) % NZ) * NC + c, x)
    left = ((y * NZ + (z + NZ - 1) % NZ) * NC + c, x)
    across = (((y + 2) % NY * NZ + z) * NC + c, x)

    def along_x(by):
        return (dp, (x + by) % NX)

    def peer(by):
        other = (q + by) % (NY * NC)
        return other, ((other // NC * NZ + z) * NC + other % NC, x)

    def send(src, dst, sem, at, device):
        return pltpu.make_async_remote_copy(
            src_ref=src, dst_ref=dst, send_sem=sem.at[(0,) + at], recv_sem=sem.at[(1,) + at],
            device_id=device, device_id_type=MESH,
        )

    page_copy = send(leave, arrive, page_sem, (), across)
    stat_copies = [send(stat.at[0], stat.at[by], stat_sem, (by,), along_x(by)) for by in (1, 2, 3)]

    def weight_copies(by):
        to = (x + by) % NX
        piece = pl.ds(to * (D // NX), D // NX)
        return [
            send(w.at[piece, :], w_in.at[by, :, pl.ds(n * HIDE, HIDE)], w_sem, (by, n), along_x(by))
            for n, w in enumerate((w_gate, w_up))
        ]

    def row_copies(g):
        out = []
        for way, device in ((0, right), (1, left)):
            src = jnp.where(g == 0, 2 * GROUPS - 1, 2 * (g - 1) + way)
            dst = 2 * g + way
            out.append(send(rows.at[src], rows.at[dst], row_sem, (g, way), device))
            out.append(send(metas.at[src], metas.at[dst], meta_sem, (g, way), device))
        return out

    def last_row_copies():
        g = GROUPS - 1
        a, b = pl.ds(0, 96), pl.ds(96, 48)
        return [
            send(rows.at[2 * g - 2, a], rows.at[2 * g, a], row_sem, (g, 0), right),
            send(rows.at[2 * g - 1, b], rows.at[2 * g, b], row_sem, (g, 1), left),
            send(metas.at[2 * g - 2], metas.at[2 * g], meta_sem, (g, 0), right),
        ]

    def taken_copy(g, by):
        other, device = peer(by)
        cls = other // NC % 2 * NC + other % NC
        return send(chosen.at[g, cls], taken.at[g, q], taken_sem, (g, by), device)

    def part_copy(ch, by):
        return send(part_out.at[ch, by], part_in.at[ch, by], part_sem, (ch, by), along_x(by))

    def hidden_copy(ch, by):
        return send(hidden.at[ch, 0], hidden.at[ch, by], hidden_sem, (ch, by), along_x(by))

    def back_copy(ch, by):
        other, device = peer(by)
        return send(back_out.at[ch, other], back_in.at[ch, q], back_sem, (ch, by), device)

    def ring_copies(j):
        return [
            send(ring_out.at[j, way], ring_in.at[j, way], ring_sem, (j, way), device)
            for way, device in ((0, right), (1, left))
        ]

    def first_ring_copies():
        a, b = pl.ds(0, 96), pl.ds(96, 48)
        return [
            send(ring_out.at[0, 0, a], ring_in.at[0, 0, a], ring_sem, (0, 0), right),
            send(ring_out.at[0, 1, b], ring_in.at[0, 1, b], ring_sem, (0, 1), left),
        ]

    own = pl.ds(x * (D // NX), D // NX)
    local = [
        pltpu.make_async_copy(w.at[own, :], w_in.at[0, :, pl.ds(n * HIDE, HIDE)], local_sem.at[n])
        for n, w in enumerate((w_gate, w_up))
    ]
    for by in range(NX):
        src = pl.ds((x + NX - by) % NX * HIDE, HIDE)
        local.append(
            pltpu.make_async_copy(w_down.at[src, :], w_out.at[pl.ds(by * HIDE, HIDE), :], local_sem.at[2 + by])
        )
    barrier = pltpu.get_barrier_semaphore()
    devices = [right, left] + [along_x(by) for by in (1, 2, 3)] + [peer(by)[1] for by in range(1, 8)]
    for device in devices:
        pl.semaphore_signal(barrier, inc=1, device_id=device, device_id_type=MESH)
    for copy in local:
        copy.start()
    stat[0] = squares[...]
    metas[2 * GROUPS - 1] = meta[...]
    ring_in[0, 0, 96:144, :] = jnp.zeros((48, WIDE), BF16)
    ring_in[0, 1, 0:96, :] = jnp.zeros((96, WIDE), BF16)
    for n in range(8):
        leave[n] = pool[out_pages[n]]
    pl.semaphore_wait(barrier, len(devices))

    for copy in stat_copies:
        copy.start()
    for by in (1, 3, 2):
        for copy in weight_copies(by):
            copy.start()

    for copy in stat_copies:
        copy.wait_recv()
    mean = (stat[0] + stat[1] + stat[2] + stat[3]) * (1.0 / D)
    scale = lax.rsqrt(mean[0:1] + EPS)
    scale = jnp.sum(token[...] * scale, axis=1, keepdims=True)
    rows[2 * GROUPS - 1] = (scaled[...] * scale).astype(BF16)
    for copy in row_copies(0):
        copy.start()
    page_copy.start()

    lane = lax.broadcasted_iota(jnp.int32, (SEL, 128), 1)

    def unpack(g):
        pair = metas[pl.ds(2 * g, 2)].reshape(64, 128)
        wide = dot(spread[...], pair)
        code = jnp.sum(jnp.where(lane == z, wide, 0.0), axis=1, keepdims=True) + base[:, 0:1]
        weight = jnp.sum(
            jnp.where((lane == z + NZ) | (lane == z + 2 * NZ), wide, 0.0), axis=1, keepdims=True
        )
        return code, weight

    def choose(g, carry):
        @pl.when(g < GROUPS - 1)
        def _():
            for copy in row_copies(g):
                copy.wait_recv()

        @pl.when(g < GROUPS - 2)
        def _():
            for copy in row_copies(g + 1):
                copy.start()

        @pl.when(g == GROUPS - 2)
        def _():
            for copy in last_row_copies():
                copy.start()

        @pl.when(g == GROUPS - 1)
        def _():
            for copy in last_row_copies():
                copy.wait_recv()

        code, _ = unpack(g)
        column = lax.broadcasted_iota(jnp.int32, (SEL, 2 * PACK), 1).astype(F32)
        hot = jnp.where(column == code, 1.0, 0.0).astype(BF16)
        picked = dot(hot, rows[pl.ds(2 * g, 2)].reshape(2 * PACK, WIDE)).astype(BF16)
        chosen[g] = picked.reshape(CLASSES, SLAB, WIDE)
        for by in range(1, 8):
            taken_copy(g, by).start()
        taken[g, q] = chosen[g, y % 2 * NC + c]
        return carry

    lax.fori_loop(0, GROUPS, choose, 0)

    for copy in local:
        copy.wait()
    for by in (1, 2, 3):
        for copy in weight_copies(by):
            copy.wait_recv()

    def first_matmul(ch):
        pieces = []
        for u in range(PER):
            g = ch * PER + u
            for by in range(1, 8):
                taken_copy(g, by).wait_recv()
            block = dot(perm[...], taken[g].reshape(NY * NC * SLAB, WIDE)).astype(BF16)
            pieces.append(
                jnp.concatenate([block[lb * ROWS : (lb + 1) * ROWS] for lb in range(LB)], axis=1)
            )
        inputs = jnp.concatenate(pieces, axis=0)
        for by in (1, 3, 2):
            part_out[ch, by] = dot(inputs, w_in[(NX - by) % NX]).astype(BF16)
            part_copy(ch, by).start()
        part_own[ch] = dot(inputs, w_in[0])

    def activate(ch):
        for by in (1, 2, 3):
            part_copy(ch, by).wait_recv()
        both = part_own[ch] + part_in[ch, 1].astype(F32) + part_in[ch, 2].astype(F32) + part_in[ch, 3].astype(F32)
        gate, upper = both[:, :HIDE], both[:, HIDE:]
        hidden[ch, 0] = (gate / (1.0 + jnp.exp(-gate)) * upper).astype(BF16)
        for by in (1, 3, 2):
            hidden_copy(ch, by).start()

    def second_matmul(ch):
        for by in (1, 2, 3):
            hidden_copy(ch, by).wait_recv()
        units = jnp.concatenate([hidden[ch, by] for by in range(NX)], axis=1)
        made = dot(units, w_out[...]).astype(BF16)
        for u in range(PER):
            part = made[u * ROWS : (u + 1) * ROWS]
            stack = jnp.concatenate([part[:, lb * WIDE : (lb + 1) * WIDE] for lb in range(LB)], axis=0)
            slabs = dot(perm_back[...], stack).astype(BF16)
            back_out[ch, :, u * SLAB : (u + 1) * SLAB, :] = slabs.reshape(NY * NC, SLAB, WIDE)
        for by in range(1, 8):
            back_copy(ch, by).start()
        back_in[ch, q] = back_out[ch, q]

    def combine(ch):
        for by in range(1, 8):
            back_copy(ch, by).wait_recv()
        for u in range(PER):
            g = ch * PER + u
            code, weight = unpack(g)
            slabs = back_in[ch, :, u * SLAB : (u + 1) * SLAB, :].astype(F32)
            both = (slabs[:CLASSES] + slabs[CLASSES:]).reshape(SEL, WIDE)
            both = (both * weight).astype(BF16)
            diagonal = lax.broadcasted_iota(jnp.int32, (SEL, SEL), 0) == lax.broadcasted_iota(
                jnp.int32, (SEL, SEL), 1
            )
            code_row = jnp.sum(jnp.where(diagonal, code, 0.0), axis=0, keepdims=True)
            place = lax.broadcasted_iota(jnp.int32, (2 * PACK, SEL), 0).astype(F32)
            hot = jnp.where(place == code_row, 1.0, 0.0).astype(BF16)
            total[g] = dot(hot, both)

    def experts(it, carry):
        @pl.when(it < CHUNKS)
        def _():
            first_matmul(it)

        @pl.when((it >= 1) & (it < CHUNKS + 1))
        def _():
            activate(it - 1)

        @pl.when((it >= 2) & (it < CHUNKS + 2))
        def _():
            second_matmul(it - 2)

        @pl.when(it >= 3)
        def _():
            combine(it - 3)

        return carry

    lax.fori_loop(0, CHUNKS + 3, experts, 0)

    scaling = 1.0 / math.sqrt(HEAD_DIM)

    def normalize(values, gain):
        mean_square = jnp.mean(values * values, axis=-1, keepdims=True)
        return values * lax.rsqrt(mean_square + EPS) * gain

    def attend(i, carry):
        pages = []
        for n in range(4):
            at = source_page[i * 4 + n]
            stayed = pool[jnp.minimum(at, 47)]
            moved = arrive[jnp.maximum(at - 48, 0)]
            pages.append(jnp.where(at < 48, stayed, moved))
        cos, sin = cosines[pl.ds(i * 16, 16)], sines[pl.ds(i * 16, 16)]
        raw = fresh[pl.ds(i * 16, 16)].astype(F32)
        keys = normalize(raw, k_gain[0:1])
        keys = keys * cos + pltpu.roll(keys, 64, axis=1) * sin
        is_key = lax.broadcasted_iota(jnp.int32, (16, 128), 0) % 2 == 0
        extra = jnp.where(is_key, keys, raw).astype(BF16)
        context = jnp.concatenate(pages + [extra, jnp.zeros((112, 128), BF16)], axis=0)
        asked = normalize(queries[pl.ds(i * 48, 48)].astype(F32), q_gain[0:1])
        cos_q = jnp.concatenate([jnp.broadcast_to(cos[2 * s : 2 * s + 1], (16, 128)) for s in range(3)], axis=0)
        sin_q = jnp.concatenate([jnp.broadcast_to(sin[2 * s : 2 * s + 1], (16, 128)) for s in range(3)], axis=0)
        asked = (asked * cos_q + pltpu.roll(asked, 64, axis=1) * sin_q).astype(BF16)
        scores = lax.dot_general(asked, context, (((1,), (1,)), ((), ())), preferred_element_type=F32) * scaling
        at = lax.broadcasted_iota(jnp.int32, (48, 640), 1)
        step = lax.broadcasted_iota(jnp.int32, (48, 640), 0) // 16
        known = at < 2 * lengths[i]
        added = (at >= 512) & (at <= 512 + 2 * step)
        valid = (known | added) & (at % 2 == 0)
        scores = jnp.where(valid, scores, -1e30)
        top = jnp.max(scores, axis=-1, keepdims=True)
        expos = jnp.where(valid, jnp.exp(scores - top), 0.0)
        probs = expos / jnp.sum(expos, axis=-1, keepdims=True)
        probs = pltpu.roll(probs, 1, axis=1).astype(BF16)
        attn[pl.ds(i * 48, 48)] = dot(probs, context).astype(BF16)
        return carry

    far = GROUPS - 1
    ring_out[0, 0] = total[far, 0:PACK].astype(BF16)
    ring_out[0, 1] = total[far, 0:PACK].astype(BF16)
    for copy in first_ring_copies():
        copy.start()
    page_copy.wait_recv()
    lax.fori_loop(0, 2, attend, 0)

    def gather_home(j, carry):
        @pl.when(j == 1)
        def _():
            for copy in first_ring_copies():
                copy.wait_recv()

        @pl.when(j > 1)
        def _():
            for copy in ring_copies(j - 1):
                copy.wait_recv()

        near = far - j
        ring_out[j, 0] = (total[near, PACK : 2 * PACK] + ring_in[j - 1, 0].astype(F32)).astype(BF16)
        ring_out[j, 1] = (total[near, 0:PACK] + ring_in[j - 1, 1].astype(F32)).astype(BF16)
        for copy in ring_copies(j):
            copy.start()

        @pl.when(j < 6)
        def _():
            lax.fori_loop(2 * j, 2 * j + 2, attend, 0)

        return carry

    lax.fori_loop(1, GROUPS, gather_home, 0)
    for copy in ring_copies(far):
        copy.wait_recv()
    moe[...] = (
        total[far, PACK : 2 * PACK] + ring_in[far, 0].astype(F32) + ring_in[far, 1].astype(F32)
    ).astype(BF16)

    page_copy.wait_send()
    for copy in stat_copies + last_row_copies() + first_ring_copies():
        copy.wait_send()
    for by in (1, 2, 3):
        for copy in weight_copies(by):
            copy.wait_send()

    def drain_pairs(g, carry):
        for by in range(1, 8):
            taken_copy(g, by).wait_send()

        @pl.when(g < GROUPS - 1)
        def _():
            for copy in row_copies(g) + ring_copies(g + 1):
                copy.wait_send()

        return carry

    def drain_chunks(ch, carry):
        for by in (1, 2, 3):
            part_copy(ch, by).wait_send()
            hidden_copy(ch, by).wait_send()
        for by in range(1, 8):
            back_copy(ch, by).wait_send()
        return carry

    lax.fori_loop(0, GROUPS, drain_pairs, 0)
    lax.fori_loop(0, CHUNKS, drain_chunks, 0)


def routing(route_ids, route_logits):
    ids = route_ids.reshape(STEPS, REQ * TOP_K)
    order = jnp.arange(REQ * TOP_K, dtype=jnp.int32)
    earlier = (ids[:, :, None] == ids[:, None, :]) & (order[None, :] < order[:, None])
    slots = jnp.sum(earlier.astype(jnp.int32), axis=2)
    target = ids * 2 + slots
    hit = target[:, :, None] == jnp.arange(128, dtype=jnp.int32)
    row = (order // TOP_K + 1)[None, :, None]
    index = jnp.sum(jnp.where(hit, row, 0), axis=1)
    index = jnp.where(index > 0, index - 1, 512).astype(F32)
    weights = jax.nn.softmax(route_logits, axis=-1).reshape(STEPS, REQ * TOP_K)
    weight = jnp.sum(jnp.where(hit, weights[:, :, None], 0.0), axis=1)
    high = lax.reduce_precision(weight, 8, 7)
    both = jnp.stack([index, high, weight - high])
    both = both.reshape(3, STEPS, 2, NZ, NC, 2).transpose(2, 4, 1, 5, 0, 3).reshape(24, 3 * NZ)
    return jnp.pad(both, ((0, 8), (0, 128 - 3 * NZ))).astype(BF16)


def local(
    q_raw, k_raw, v_raw, q_gain, k_gain, kv_pool, page_table, cache_len, out_pages, in_slots,
    hidden_in, ln_gain, route_ids, route_logits, w_gate, w_up, w_down,
):
    x = lax.axis_index("rep")
    spread, base, perm, token = tables()
    flat = page_table.reshape(-1)
    match = flat[:, None] == in_slots[None, :]
    source = jnp.where(
        jnp.any(match, axis=1), 48 + jnp.sum(jnp.where(match, jnp.arange(8, dtype=jnp.int32), 0), axis=1), flat
    )
    values = hidden_in.astype(F32)
    gain = lax.dynamic_slice(ln_gain, (x * (D // NX),), (D // NX,))
    scaled = (values * gain).reshape(STEPS, REQ, LB, WIDE).transpose(0, 2, 1, 3).reshape(PACK, WIDE)
    squares = jnp.sum(values * values, axis=-1).reshape(1, STEPS * REQ)
    squares = jnp.broadcast_to(jnp.pad(squares, ((0, 0), (0, 128 - STEPS * REQ))), (8, 128))
    meta = routing(route_ids, route_logits)
    pool = kv_pool.reshape(48, 128, HEAD_DIM)
    queries = q_raw.reshape(STEPS, REQ, 16, HEAD_DIM).transpose(1, 0, 2, 3).reshape(REQ * 48, HEAD_DIM)
    fresh = jnp.stack([k_raw, v_raw], axis=2).transpose(1, 0, 2, 3).reshape(REQ, 6, HEAD_DIM)
    fresh = jnp.pad(fresh, ((0, 0), (0, 10), (0, 0))).reshape(REQ * 16, HEAD_DIM)
    exponent = jnp.arange(HEAD_DIM // 2, dtype=F32) * (2.0 / HEAD_DIM)
    frequency = THETA ** (-exponent)
    place = jnp.arange(16, dtype=jnp.int32) // 2
    position = (cache_len[:, None] + place[None, :]).astype(F32).reshape(-1)
    angle = position[:, None] * frequency[None, :]
    cosine, sine = jnp.cos(angle), jnp.sin(angle)
    cosines = jnp.concatenate([cosine, cosine], axis=1)
    sines = jnp.concatenate([-sine, sine], axis=1)
    rows_of = lambda g: jnp.broadcast_to(g[None, :], (8, HEAD_DIM))

    smem = pl.BlockSpec(memory_space=pltpu.SMEM)
    vmem = pl.BlockSpec(memory_space=pltpu.VMEM)
    anywhere = pl.BlockSpec(memory_space=pl.ANY)
    peers = NY * NC
    sem = pltpu.SemaphoreType.DMA
    attn, moe = pl.pallas_call(
        kernel,
        out_shape=(
            jax.ShapeDtypeStruct((REQ * 48, HEAD_DIM), BF16),
            jax.ShapeDtypeStruct((PACK, WIDE), BF16),
        ),
        in_specs=[smem] * 3 + [vmem] * 15 + [anywhere] * 3,
        out_specs=(vmem, vmem),
        scratch_shapes=[
            pltpu.VMEM((8, 128, HEAD_DIM), BF16),
            pltpu.VMEM((8, 128, HEAD_DIM), BF16),
            pltpu.VMEM((NX, 8, 128), F32),
            pltpu.VMEM((NZ, PACK, WIDE), BF16),
            pltpu.VMEM((NZ, 32, 128), BF16),
            pltpu.VMEM((GROUPS, CLASSES, SLAB, WIDE), BF16),
            pltpu.VMEM((GROUPS, peers, SLAB, WIDE), BF16),
            pltpu.VMEM((NX, D // NX, 2 * HIDE), BF16),
            pltpu.VMEM((NX * HIDE, D // NX), BF16),
            pltpu.VMEM((CHUNKS, PER * ROWS, 2 * HIDE), F32),
            pltpu.VMEM((CHUNKS, NX, PER * ROWS, 2 * HIDE), BF16),
            pltpu.VMEM((CHUNKS, NX, PER * ROWS, 2 * HIDE), BF16),
            pltpu.VMEM((CHUNKS, NX, PER * ROWS, HIDE), BF16),
            pltpu.VMEM((CHUNKS, peers, PER * SLAB, WIDE), BF16),
            pltpu.VMEM((CHUNKS, peers, PER * SLAB, WIDE), BF16),
            pltpu.VMEM((GROUPS, 2 * PACK, WIDE), F32),
            pltpu.VMEM((GROUPS, 2, PACK, WIDE), BF16),
            pltpu.VMEM((GROUPS, 2, PACK, WIDE), BF16),
            sem((6,)),
            sem((2,)),
            sem((2, NX)),
            sem((2, NX, 2)),
            sem((2, GROUPS, 2)),
            sem((2, GROUPS, 2)),
            sem((2, GROUPS, peers)),
            sem((2, CHUNKS, NX)),
            sem((2, CHUNKS, NX)),
            sem((2, CHUNKS, peers)),
            sem((2, GROUPS, 2)),
        ],
        compiler_params=pltpu.CompilerParams(
            collective_id=0, has_side_effects=True, vmem_limit_bytes=48 * 1024 * 1024
        ),
    )(
        source, out_pages, cache_len,
        scaled, squares, meta, pool, queries, fresh, cosines, sines, rows_of(q_gain), rows_of(k_gain),
        jnp.asarray(spread, BF16), jnp.asarray(base), jnp.asarray(perm, BF16), jnp.asarray(perm.T, BF16),
        jnp.asarray(token),
        w_gate.reshape(D, HIDE), w_up.reshape(D, HIDE), w_down.reshape(NX * HIDE, D // NX),
    )
    attn = attn.reshape(REQ, STEPS, 16, HEAD_DIM).transpose(1, 0, 2, 3).reshape(STEPS, REQ, 16 * HEAD_DIM)
    moe = moe.reshape(STEPS, LB, REQ, WIDE).transpose(0, 2, 1, 3).reshape(STEPS, REQ, D // NX)
    return attn, moe


def solution(mesh):
    return jax.shard_map(
        local,
        mesh=mesh,
        in_specs=(
            P(None, "dp", "rep"),
            P(None, "dp", "rep"),
            P(None, "dp", "rep"),
            P(),
            P(),
            P("dp", None, None, "rep"),
            P("dp", None),
            P("dp"),
            P("dp"),
            P("dp"),
            P(None, "dp", "rep"),
            P(),
            P(None, "dp", None),
            P(None, "dp", None),
            P("dp", None, "rep"),
            P("dp", None, "rep"),
            P("dp", None, "rep"),
        ),
        out_specs=(P(None, "dp", "rep"), P(None, "dp", "rep")),
        check_vma=False,
    )
```

time: 593 us -> 152 us (0.26)
  the two profiles are of different devices: /device:TPU:1 before, /device:TPU:2 now
where the time goes in v1:
time: 152 us; the launch traced here: 151 us
  Pallas kernels  120 us (79%)
  local copies, waits for them, and re-layouts  23.2 us (15%)
  other arithmetic  6.38 us (4%)
    pallas_call x1, Pallas kernels, local(): pl.pallas_call(kernel, out_shape=(jax.ShapeDtypeStruct((REQ * 48, HEAD_DI...  120 us
    unnamed x30, local copies, waits for them, and re-layouts  8.92 us
    reshape x3, local copies, waits for them, and re-layouts, local(): (values * gain).reshape(STEPS, REQ, LB, WIDE).transpose(0, 2, 1, 3)  3.29 us

profile of v1, /device:TPU:2, one launch (start us, length us, event | category | flops | bytes accessed | tf_op | source)
XLA Modules:
  0.0 150.9 jit_solution(6242495987505430074)
XLA Ops:
  0.6 0.8 copy.72
  1.8 0.8 fusion.8
  4.1 0.9 add_convert_fusion
  5.5 0.7 pad_maximum_fusion
  7.0 0.7 reshape.200
  7.7 1.6 %copy.83 = f32[3,12,4,256]{3,1,2,0:T(8,128)} copy(f32[3,12,4,256]{3,2,1,0:T(4,128)} %reshape.200) | data formatting | bytes 294912 | tf_op jit(solution)/shard_map/reshape | solution.py:455
  9.4 0.9 reshape.201.scaled
  10.4 0.8 copy.70
  11.3 0.7 compare_reduce_fusion
  12.0 0.7 fusion.6
  13.3 1.7 %reshape.206 = bf16[3,12,16,128]{3,2,1,0:T(8,128)(2,1)} reshape(bf16[3,12,2048]{2,1,0:T(8,128)(2,1)} %param.22) | data formatting | bytes 294912 | tf_op jit(solution)/shard_map/reshape | solution.py:460
  15.0 0.9 copy.78
  15.9 0.7 maximum_bitcast_fusion
  17.3 1.3 reshape.208
  18.6 0.7 pad.15
  20.7 0.9 copy-done.3
  21.6 1.0 copy-done.4
  22.5 1.0 copy-done.5
  23.5 0.9 copy-done.6
  24.4 0.9 copy-done.8
  25.3 0.8 copy-done.9
  27.4 120.4 %shard_map.221 = (bf16[576,128]{1,0:T(8,128)(2,1)S(1)}, bf16[144,256]{1,0:T(8,128)(2,1)S(1)}) custom-call(s32[48]{0:T(128)S(1)} %copy-done.11, s32[8]{0:T(128)S(1)} %copy-done.12, s32[12]{0:T(128)S(1)} %copy-done.10, f32[144,256]{1,0:T(8,128)S(1)} %reshape.201.scaled, f32[8,128]{1,0:T(8,128)S(1)} %broadcast_in_dim.73.squares, bf16[32,128]{1,0:T(8,128)(2,1)S(1)} %pad.14.meta, ...), custom_call_target="tpu_custom_call" | custom-call | tf_op jit(solution)/shard_map/pallas_call | solution.py:478
  148.5 0.8 reshape.214
  149.2 0.9 reshape.215
  (59 shorter events, 8.3 us)
Async XLA Ops:
  0.6 6.3 %copy-start.13 = (bf16[3,12,1024]{2,1,0:T(8,128)(2,1)S(1)}, bf16[3,12,1024]{2,1,0:T(8,128)(2,1)}, u32[]{:S(2)}) copy-start(bf16[3,12,1024]{2,1,0:T(8,128)(2,1)} %param.32) | copy-start | bytes 221188
  3.9 16.8 %copy-start.2 = (bf16[1,512,1024]{2,1,0:T(8,128)(2,1)S(1)}, bf16[1,512,1024]{2,1,0:T(8,128)(2,1)}, u32[]{:S(2)}) copy-start(bf16[1,512,1024]{2,1,0:T(8,128)(2,1)} %param.38) | copy-start | bytes 3145732
  3.9 16.8 %copy-start = (bf16[1,4096,128]{2,1,0:T(8,128)(2,1)S(1)}, bf16[1,4096,128]{2,1,0:T(8,128)(2,1)}, u32[]{:S(2)}) copy-start(bf16[1,4096,128]{2,1,0:T(8,128)(2,1)} %param.36) | copy-start | bytes 3145732
  3.9 16.7 %copy-start.1 = (bf16[1,4096,128]{2,1,0:T(8,128)(2,1)S(1)}, bf16[1,4096,128]{2,1,0:T(8,128)(2,1)}, u32[]{:S(2)}) copy-start(bf16[1,4096,128]{2,1,0:T(8,128)(2,1)} %param.37) | copy-start | bytes 3145732
  3.9 16.7 %copy-start.10 = (s32[12]{0:T(128)S(1)}, s32[12]{0:T(128)}, u32[]{:S(2)}) copy-start(s32[12]{0:T(128)} %lengths.1) | copy-start | bytes 148
  20.7 0.9 copy-start.3
  21.6 1.0 copy-start.4
  22.5 1.0 copy-start.5
  23.5 0.9 copy-start.6
  24.4 0.9 copy-start.8
  25.3 0.8 copy-start.9
  26.1 0.6 copy-start.11
  26.7 0.7 copy-start.12
  147.8 0.6 copy-start.7

commit v2 on v1

v2 whole, which is shorter than its diff:
```python
import functools
import math

import jax
import jax.numpy as jnp
import numpy as np
from jax import lax
from jax.experimental import pallas as pl
from jax.experimental.pallas import tpu as pltpu
from jax.sharding import PartitionSpec as P

NX, NY, NZ, NC = 4, 4, 16, 2
STEPS, REQ, TOP_K = 3, 12, 8
D, HEAD_DIM = 4096, 128
EPS = 1e-06
THETA = 1000000.0

LB = 4
PACK = STEPS * LB * REQ
BLOCK = PACK + 16
WIDE = D // NX // LB
STRIDE = 4
CHUNKS = STRIDE
PER = NZ // STRIDE // 2
NEAR = (0, 1, -1, 2)
FIRST, SECOND = 4, 8
SLAB = LB * 2 * STEPS * 2
ROWS = SLAB // LB * NY * NC
CLASSES = 4
SEL = CLASSES * SLAB
HIDE = 128
MESH = pl.DeviceIdType.MESH
F32, BF16 = jnp.float32, jnp.bfloat16


def tables():
    peers, per = NY * NC, SLAB // LB
    out = np.full((peers * SLAB + 8, 128), -1, np.float32)
    row = 0
    for cls in range(CLASSES):
        for lb in range(LB):
            for zz in range(2):
                for s in range(STEPS):
                    for slot in range(2):
                        out[row, 4] = zz * PACK + s * LB * REQ + lb * REQ
                        out[row, 5] = zz * 32 + cls * 8 + s * 2 + slot
                        row += 1
    for lb in range(LB):
        for q in range(peers):
            for r in range(per):
                a, b = (lb * peers + q) * per + r, q * SLAB + lb * per + r
                out[a, 0], out[b, 1] = b, a
    for s in range(STEPS):
        for lb in range(LB):
            for i in range(REQ):
                a, b = (s * LB + lb) * REQ + i, lb * 48 + s * 16 + i
                out[a, 2], out[b, 3] = b, a
    exponent = np.arange(HEAD_DIM // 2, dtype=np.float32) * np.float32(2.0 / HEAD_DIM)
    frequency = np.power(np.float32(THETA), -exponent).astype(np.float32)
    out[peers * SLAB :] = np.concatenate([frequency, frequency])
    return out


def dot(a, b):
    return jnp.dot(a, b, preferred_element_type=F32)


def iota(shape, axis):
    return lax.broadcasted_iota(jnp.int32, shape, axis)


def one_hot(column, width):
    at = iota((column.shape[0], width), 1).astype(F32)
    return jnp.where(at == column, 1.0, 0.0).astype(BF16)


def kernel(
    q_hbm, k_hbm, v_hbm, q_gain_hbm, k_gain_hbm, pool_hbm, table_hbm, len_hbm, out_hbm, slots_hbm,
    hid_hbm, ln_hbm, ids_hbm, logits_hbm, w_gate, w_up, w_down, const_hbm,
    attn, moe,
    q_in, k_in, v_in, q_gain, k_gain, pool, page_table, lengths, out_pages, in_slots,
    hid, ln_gain, ids, logits, const,
    spread, perm, perm_back, pack, unpack_rows, q_rows, k_rows, v_rows, cosines, sines, attn_rows,
    natural, leave, arrive, stat, rows, chosen, taken, w_in, w_out,
    part_own, part_out, part_in, hidden, back_out, back_in, kept, home_out, home_in, last_out, last_in,
    local_sem, load_sem, page_sem, stat_sem, w_sem, row_sem, taken_sem,
    part_sem, hidden_sem, back_sem, home_sem, last_sem,
):
    dp, x = lax.axis_index("dp"), lax.axis_index("rep")
    y, z, c = dp // (NZ * NC), (dp // NC) % NZ, dp % NC
    q = y * NC + c
    mine = z // STRIDE
    across = (((y + 2) % NY * NZ + z) * NC + c, x)

    def along_x(by):
        return (dp, (x + by) % NX)

    def along_z(by):
        return ((y * NZ + (z + by + NZ) % NZ) * NC + c, x)

    def peer(by):
        other = (q + by) % (NY * NC)
        return other, ((other // NC * NZ + z) * NC + other % NC, x)

    def send(src, dst, sem, at, device):
        return pltpu.make_async_remote_copy(
            src_ref=src, dst_ref=dst, send_sem=sem.at[(0,) + at], recv_sem=sem.at[(1,) + at],
            device_id=device, device_id_type=MESH,
        )

    def page_copy():
        return send(leave, arrive, page_sem, (), across)

    def stat_copies():
        return [send(stat.at[0], stat.at[by], stat_sem, (by,), along_x(by)) for by in (1, 2, 3)]

    def weight_copies(by):
        to = (x + by) % NX
        piece = pl.ds(to * (D // NX), D // NX)
        return [
            send(w.at[piece, :], w_in.at[by, :, pl.ds(n * HIDE, HIDE)], w_sem, (by, n), along_x(by))
            for n, w in enumerate((w_gate, w_up))
        ]

    def far_copies():
        return [
            send(rows.at[mine], rows.at[mine], row_sem, (a,), along_z(-STRIDE * a)) for a in (1, 2, 3)
        ]

    def near_copies(n):
        if n < 3:
            pieces = ((pl.ds(0, STRIDE), pl.ds(STRIDE * n, STRIDE), 3 + n, -NEAR[n]),)
        else:
            pieces = ((pl.ds(0, 2), pl.ds(12, 2), 6, -2), (pl.ds(2, 2), pl.ds(14, 2), 7, 2))
        return [send(rows.at[a], rows.at[b], row_sem, (at,), along_z(by)) for a, b, at, by in pieces]

    def taken_copy(ch, by):
        other, device = peer(by)
        cls = other // NC % 2 * NC + other % NC
        return send(chosen.at[ch, cls], taken.at[ch, q], taken_sem, (ch, by), device)

    def part_copy(ch, by):
        return send(part_out.at[ch, by], part_in.at[ch, by], part_sem, (ch, by), along_x(by))

    def hidden_copy(ch, by):
        return send(hidden.at[ch, 0], hidden.at[ch, by], hidden_sem, (ch, by), along_x(by))

    def back_copy(ch, by):
        other, device = peer(by)
        return send(back_out.at[ch, other], back_in.at[ch, q], back_sem, (ch, by), device)

    def home_copies(n):
        if n < 3:
            return [send(home_out.at[n], home_in.at[n], home_sem, (n,), along_z(NEAR[n]))]
        return [
            send(home_out.at[3, at], home_in.at[3, at], home_sem, (3 + m,), along_z(by))
            for m, (at, by) in enumerate(((pl.ds(0, 2), 2), (pl.ds(2, 2), -2)))
        ]

    def last_copy(a):
        return send(last_out.at[a], last_in.at[a], last_sem, (a,), along_z(STRIDE * a))

    loads = {
        name: pltpu.make_async_copy(src, dst, load_sem.at[n])
        for n, (name, src, dst) in enumerate((
            ("hid", hid_hbm, hid), ("out", out_hbm, out_pages), ("pool", pool_hbm, pool),
            ("ln", ln_hbm, ln_gain), ("ids", ids_hbm, ids), ("logits", logits_hbm, logits),
            ("const", const_hbm, const), ("len", len_hbm, lengths), ("table", table_hbm, page_table),
            ("slots", slots_hbm, in_slots), ("k", k_hbm, k_in), ("v", v_hbm, v_in),
            ("k_gain", k_gain_hbm, k_gain), ("q_gain", q_gain_hbm, q_gain), ("q", q_hbm, q_in),
        ))
    }
    for copy in loads.values():
        copy.start()
    own = pl.ds(x * (D // NX), D // NX)
    local = [
        pltpu.make_async_copy(w.at[own, :], w_in.at[0, :, pl.ds(n * HIDE, HIDE)], local_sem.at[n])
        for n, w in enumerate((w_gate, w_up))
    ]
    for by in range(NX):
        src = pl.ds((x + NX - by) % NX * HIDE, HIDE)
        local.append(
            pltpu.make_async_copy(w_down.at[src, :], w_out.at[pl.ds(by * HIDE, HIDE), :], local_sem.at[2 + by])
        )
    barrier = pltpu.get_barrier_semaphore()
    devices = [along_z(by) for by in (1, -1, 2, -2, 4, -4, 8)]
    devices += [along_x(by) for by in (1, 2, 3)] + [peer(by)[1] for by in range(1, 8)]
    for device in devices:
        pl.semaphore_signal(barrier, inc=1, device_id=device, device_id_type=MESH)
    for copy in local:
        copy.start()
    loads["hid"].wait()
    stat[0] = jnp.zeros((STEPS, 16, 128), F32)
    natural[...] = jnp.zeros((STEPS * 16, D // NX), BF16)
    for s in range(STEPS):
        values = hid[s].astype(F32)
        square = jnp.sum(values * values, axis=1, keepdims=True)
        stat[0, s, 0:REQ, :] = jnp.broadcast_to(square, (REQ, 128))
    pl.semaphore_wait(barrier, len(devices))

    for copy in stat_copies():
        copy.start()
    for by in (1, 3, 2):
        for copy in weight_copies(by):
            copy.start()
    loads["out"].wait()
    loads["pool"].wait()
    for n in range(8):
        leave[n] = pool[out_pages[n]]
    page_copy().start()

    for name in ("ln", "ids", "logits", "const"):
        loads[name].wait()
    expert, token = iota((64, REQ), 0), iota((64, REQ), 1).astype(F32)
    lane = iota((64, 128), 1)
    parts = [jnp.zeros((64, 128), F32) for _ in range(3)]
    for s in range(STEPS):
        raw = logits[s]
        expo = jnp.exp(raw - jnp.max(raw, axis=0, keepdims=True))
        share = expo / jnp.sum(expo, axis=0, keepdims=True)
        named = jnp.zeros((64, REQ), F32)
        weight = jnp.zeros((64, REQ), F32)
        for k in range(TOP_K):
            hit = ids[s, k : k + 1, :] == expert
            named = jnp.where(hit, 1.0, named)
            weight = jnp.where(hit, share[k : k + 1, :], weight)
        first = jnp.min(jnp.where(named > 0, token, 512.0), axis=1, keepdims=True)
        second = jnp.max(jnp.where(named > 0, token, -1.0), axis=1, keepdims=True)
        second = jnp.where(second > first, second, 512.0)
        for slot, row in ((0, first), (1, second)):
            given = jnp.sum(jnp.where(token == row, weight, 0.0), axis=1, keepdims=True)
            high = given.astype(BF16).astype(F32)
            for n, column in enumerate((row, high, given - high)):
                parts[n] = jnp.where(lane == 2 * s + slot, column, parts[n])
    turned = jnp.transpose(jnp.concatenate(parts + [jnp.zeros((64, 128), F32)], axis=0))[0:8].astype(BF16)
    place, lane = iota((256, 128), 0), iota((256, 128), 1)
    part = place // 64
    here = (lane // NZ == part) & (part < 3)
    blocks = []
    for cls in range(CLASSES):
        wanted = (cls // NC) * 32 + cls % NC + 2 * (lane % NZ)
        blocks.append(dot(turned, jnp.where(here & (place % 64 == wanted), 1.0, 0.0).astype(BF16)))
    for half in range(2):
        rows[mine, PACK:BLOCK, half * 128 : half * 128 + 128] = jnp.concatenate(
            blocks[2 * half : 2 * half + 2], axis=0
        ).astype(BF16)
    pack[...] = one_hot(const[0:PACK, 2:3], LB * 48)

    for copy in stat_copies():
        copy.wait_recv()
    gain_rows = ln_gain[pl.ds(x * 8, 8), :]
    gain = jnp.concatenate([gain_rows[n : n + 1] for n in range(8)], axis=1)
    for s in range(STEPS):
        mean = (stat[0, s] + stat[1, s] + stat[2, s] + stat[3, s]) * (1.0 / D)
        scale = lax.rsqrt(mean[0:REQ, 0:1] + EPS)
        natural[s * 16 : s * 16 + REQ, :] = (hid[s].astype(F32) * scale * gain).astype(BF16)
    whole = natural[...]
    stack = jnp.concatenate([whole[:, lb * WIDE : (lb + 1) * WIDE] for lb in range(LB)], axis=0)
    rows[mine, 0:PACK, :] = dot(pack[...], stack).astype(BF16)
    for copy in far_copies():
        copy.start()

    spread[...] = one_hot(const[0:SEL, 5:6], 64)
    perm[...] = one_hot(const[0 : NY * NC * SLAB, 0:1], NY * NC * SLAB)
    perm_back[...] = one_hot(const[0 : NY * NC * SLAB, 1:2], NY * NC * SLAB)
    unpack_rows[...] = one_hot(const[0 : LB * 48, 3:4], PACK)
    for name in ("len", "k", "v", "k_gain", "q_gain", "q", "table", "slots"):
        loads[name].wait()

    def normalize(values, gain):
        mean_square = jnp.mean(values * values, axis=-1, keepdims=True)
        return values * lax.rsqrt(mean_square + EPS) * gain

    request = iota((16, 128), 0)
    start = jnp.zeros((16, 128), jnp.int32)
    for i in range(REQ):
        start = jnp.where(request == i, lengths[i], start)
    sign = jnp.where(iota((16, 128), 1) < 64, -1.0, 1.0)
    frequency = const[NY * NC * SLAB : NY * NC * SLAB + 1, :]
    for s in range(STEPS):
        angle = (start + s).astype(F32) * frequency
        cosines[s] = jnp.cos(angle)
        sines[s] = jnp.sin(angle) * sign
        keys = normalize(k_in[s].astype(F32), k_gain[...])
        k_rows[s, 0:REQ, :] = keys * cosines[s, 0:REQ] + pltpu.roll(keys, 64, axis=1) * sines[s, 0:REQ]
        v_rows[s, 0:REQ, :] = v_in[s].astype(F32)
        q_rows[s, 0:REQ, :] = q_in[s].astype(F32)

    def unpack(g):
        pair = rows[pl.ds(2 * g, 2), PACK:BLOCK, :]
        pair = jnp.concatenate([pair[zz, :, h * 128 : h * 128 + 128] for zz in range(2) for h in range(2)], axis=0)
        wide = dot(spread[...], pair)
        lane = iota((SEL, 128), 1)
        code = jnp.sum(jnp.where(lane == z, wide, 0.0), axis=1, keepdims=True) + const[0:SEL, 4:5]
        weight = jnp.sum(
            jnp.where((lane == z + NZ) | (lane == z + 2 * NZ), wide, 0.0), axis=1, keepdims=True
        )
        return code, weight

    def choose(ch):
        for u in range(PER):
            g = ch * PER + u
            code, _ = unpack(g)
            picked = dot(one_hot(code, 2 * PACK), rows[pl.ds(2 * g, 2), 0:PACK, :].reshape(2 * PACK, WIDE)).astype(BF16)
            chosen[ch, :, u * SLAB : (u + 1) * SLAB, :] = picked.reshape(CLASSES, SLAB, WIDE)
        for by in range(1, 8):
            taken_copy(ch, by).start()
        taken[ch, q] = chosen[ch, y % 2 * NC + c]

    scaling = 1.0 / math.sqrt(HEAD_DIM)

    def attend(i, carry):
        pages = []
        for n in range(4):
            at = page_table[n, i]
            moved_to = at
            for m in range(8):
                moved_to = jnp.where(in_slots[m] == at, 48 + m, moved_to)
            pages.append(jnp.where(moved_to < 48, pool[at], arrive[jnp.maximum(moved_to - 48, 0)]))
        row = iota((16, 128), 0)
        extra = jnp.zeros((16, 128), F32)
        asked, cos, sin = [], [], []
        for s in range(STEPS):
            extra = jnp.where(row == 2 * s, k_rows[s, pl.ds(i, 1), :], extra)
            extra = jnp.where(row == 2 * s + 1, v_rows[s, pl.ds(i, 1), :], extra)
            line = q_rows[s, pl.ds(i, 1), :]
            asked += [line[:, h * HEAD_DIM : (h + 1) * HEAD_DIM] for h in range(16)]
            cos.append(jnp.broadcast_to(cosines[s, pl.ds(i, 1), :], (16, 128)))
            sin.append(jnp.broadcast_to(sines[s, pl.ds(i, 1), :], (16, 128)))
        context = jnp.concatenate(pages + [extra.astype(BF16), jnp.zeros((112, 128), BF16)], axis=0)
        asked = normalize(jnp.concatenate(asked, axis=0), q_gain[...])
        asked = asked * jnp.concatenate(cos, axis=0) + pltpu.roll(asked, 64, axis=1) * jnp.concatenate(sin, axis=0)
        scores = lax.dot_general(
            asked.astype(BF16), context, (((1,), (1,)), ((), ())), preferred_element_type=F32
        ) * scaling
        at, step = iota((48, 640), 1), iota((48, 640), 0) // 16
        known = at < 2 * lengths[i]
        added = (at >= 512) & (at <= 512 + 2 * step)
        valid = (known | added) & (at % 2 == 0)
        scores = jnp.where(valid, scores, -1e30)
        top = jnp.max(scores, axis=-1, keepdims=True)
        expos = jnp.where(valid, jnp.exp(scores - top), 0.0)
        probs = expos / jnp.sum(expos, axis=-1, keepdims=True)
        probs = pltpu.roll(probs, 1, axis=1).astype(BF16)
        mixed = dot(probs, context)
        for s in range(STEPS):
            attn_rows[s, pl.ds(i, 1), :] = jnp.concatenate(
                [mixed[s * 16 + h : s * 16 + h + 1] for h in range(16)], axis=1
            )
        return carry

    for copy in far_copies():
        copy.wait_recv()
    for n in (1, 2, 3):
        for copy in near_copies(n):
            copy.start()
    choose(0)
    page_copy().wait_recv()
    lax.fori_loop(0, FIRST, attend, 0)

    def choose_next(ch, carry):
        for n in (1, 2, 3):
            @pl.when(jnp.int32(ch) == n)
            def _(n=n):
                for copy in near_copies(n):
                    copy.wait_recv()

        choose(ch)
        return carry

    lax.fori_loop(1, CHUNKS - 1, choose_next, 0)

    for copy in local:
        copy.wait()
    for by in (1, 2, 3):
        for copy in weight_copies(by):
            copy.wait_recv()

    def first_matmul(ch):
        for by in range(1, 8):
            taken_copy(ch, by).wait_recv()
        pieces = []
        for u in range(PER):
            slabs = taken[ch, :, u * SLAB : (u + 1) * SLAB, :].reshape(NY * NC * SLAB, WIDE)
            block = dot(perm[...], slabs).astype(BF16)
            pieces.append(
                jnp.concatenate([block[lb * ROWS : (lb + 1) * ROWS] for lb in range(LB)], axis=1)
            )
        inputs = jnp.concatenate(pieces, axis=0)
        for by in (2, 1, 3):
            part_out[ch, by] = dot(inputs, w_in[(NX - by) % NX]).astype(BF16)
            part_copy(ch, by).start()
        part_own[ch] = dot(inputs, w_in[0])

    def activate(ch):
        for by in (1, 2, 3):
            part_copy(ch, by).wait_recv()
        both = part_own[ch] + part_in[ch, 1].astype(F32) + part_in[ch, 2].astype(F32) + part_in[ch, 3].astype(F32)
        gate, upper = both[:, :HIDE], both[:, HIDE:]
        hidden[ch, 0] = (gate / (1.0 + jnp.exp(-gate)) * upper).astype(BF16)
        for by in (2, 1, 3):
            hidden_copy(ch, by).start()

    def second_matmul(ch):
        for by in (1, 2, 3):
            hidden_copy(ch, by).wait_recv()
        units = jnp.concatenate([hidden[ch, by] for by in range(NX)], axis=1)
        made = dot(units, w_out[...]).astype(BF16)
        for u in range(PER):
            part = made[u * ROWS : (u + 1) * ROWS]
            stack = jnp.concatenate([part[:, lb * WIDE : (lb + 1) * WIDE] for lb in range(LB)], axis=0)
            slabs = dot(perm_back[...], stack).astype(BF16)
            back_out[ch, :, u * SLAB : (u + 1) * SLAB, :] = slabs.reshape(NY * NC, SLAB, WIDE)
        for by in range(1, 8):
            back_copy(ch, by).start()
        back_in[ch, q] = back_out[ch, q]

    def combine(ch):
        for by in range(1, 8):
            back_copy(ch, by).wait_recv()
        for u in range(PER):
            g = ch * PER + u
            code, weight = unpack(g)
            slabs = back_in[ch, :, u * SLAB : (u + 1) * SLAB, :].astype(F32)
            both = (slabs[:CLASSES] + slabs[CLASSES:]).reshape(SEL, WIDE)
            both = (both * weight).astype(BF16)
            diagonal = iota((SEL, SEL), 0) == iota((SEL, SEL), 1)
            code_row = jnp.sum(jnp.where(diagonal, code, 0.0), axis=0, keepdims=True)
            at = iota((2 * PACK, SEL), 0).astype(F32)
            sums = dot(jnp.where(at == code_row, 1.0, 0.0).astype(BF16), both)
            home_out[ch, 2 * u : 2 * u + 2] = sums.astype(BF16).reshape(2, PACK, WIDE)

            @pl.when(ch == 0)
            def _(u=u, sums=sums):
                kept[2 * u : 2 * u + 2] = sums.reshape(2, PACK, WIDE)

        for n in (1, 2, 3):
            @pl.when(ch == n)
            def _(n=n):
                for copy in home_copies(n):
                    copy.start()

    def experts(it, carry):
        @pl.when(it == 1)
        def _():
            choose_next(CHUNKS - 1, 0)

        @pl.when(it < CHUNKS)
        def _():
            first_matmul((it + 1) % CHUNKS)

        @pl.when((it >= 1) & (it < CHUNKS + 1))
        def _():
            activate(it % CHUNKS)

        @pl.when((it >= 2) & (it < CHUNKS + 2))
        def _():
            second_matmul((it - 1) % CHUNKS)

        @pl.when(it >= 3)
        def _():
            combine((it - 2) % CHUNKS)

        return carry

    lax.fori_loop(0, CHUNKS + 3, experts, 0)

    lax.fori_loop(FIRST, SECOND, attend, 0)
    for n in (1, 2, 3):
        for copy in home_copies(n):
            copy.wait_recv()

    def gathered(a):
        at = (mine + a) % STRIDE
        summed = kept[at]
        for n in (1, 2, 3):
            summed = summed + home_in[n, at].astype(F32)
        return summed

    for a in (2, 1, 3):
        last_out[a] = gathered(a).astype(BF16)
        last_copy(a).start()
    lax.fori_loop(SECOND, REQ, attend, 0)
    for s in range(STEPS):
        attn[s] = attn_rows[s, 0:REQ, :].astype(BF16)
    for a in (1, 2, 3):
        last_copy(a).wait_recv()
    summed = gathered(0)
    for a in (1, 2, 3):
        summed = summed + last_in[a].astype(F32)
    flat = dot(unpack_rows[...], summed.astype(BF16)).astype(BF16)
    for s in range(STEPS):
        moe[s] = jnp.concatenate(
            [flat[lb * 48 + s * 16 : lb * 48 + s * 16 + 16] for lb in range(LB)], axis=1
        )[0:REQ]

    page_copy().wait_send()
    for copy in stat_copies() + far_copies():
        copy.wait_send()
    for n in (1, 2, 3):
        for copy in weight_copies(n) + near_copies(n) + home_copies(n) + [last_copy(n)]:
            copy.wait_send()

    def drain(ch, carry):
        for by in (1, 2, 3):
            part_copy(ch, by).wait_send()
            hidden_copy(ch, by).wait_send()
        for by in range(1, 8):
            taken_copy(ch, by).wait_send()
            back_copy(ch, by).wait_send()
        return carry

    lax.fori_loop(0, CHUNKS, drain, 0)


def local(
    q_raw, k_raw, v_raw, q_gain, k_gain, kv_pool, page_table, cache_len, out_pages, in_slots,
    hidden_in, ln_gain, route_ids, route_logits, w_gate, w_up, w_down,
):
    hbm = pl.BlockSpec(memory_space=pltpu.HBM)
    vmem = pl.BlockSpec(memory_space=pltpu.VMEM)
    peers, part = NY * NC, D // NX
    sem, buf = pltpu.SemaphoreType.DMA, pltpu.VMEM
    const = tables()
    operands = (
        q_raw, k_raw, v_raw, q_gain.reshape(1, HEAD_DIM), k_gain.reshape(1, HEAD_DIM),
        kv_pool.reshape(48, 128, HEAD_DIM), page_table.T, cache_len, out_pages, in_slots,
        hidden_in, ln_gain.reshape(D // 128, 128), route_ids.transpose(0, 2, 1), route_logits.transpose(0, 2, 1),
        w_gate.reshape(D, HIDE), w_up.reshape(D, HIDE), w_down.reshape(NX * HIDE, part), jnp.asarray(const),
    )
    held = [
        pltpu.SMEM(a.shape, a.dtype) if n in (6, 7, 8, 9) else buf(a.shape, a.dtype)
        for n, a in enumerate(operands)
        if n not in (14, 15, 16)
    ]
    attn, moe = pl.pallas_call(
        kernel,
        out_shape=(
            jax.ShapeDtypeStruct((STEPS, REQ, 16 * HEAD_DIM), BF16),
            jax.ShapeDtypeStruct((STEPS, REQ, part), BF16),
        ),
        in_specs=[hbm] * len(operands),
        out_specs=(vmem, vmem),
        scratch_shapes=held + [
            buf((SEL, 64), BF16),
            buf((peers * SLAB, peers * SLAB), BF16),
            buf((peers * SLAB, peers * SLAB), BF16),
            buf((PACK, LB * 48), BF16),
            buf((LB * 48, PACK), BF16),
            buf((STEPS, 16, 16 * HEAD_DIM), F32),
            buf((STEPS, 16, HEAD_DIM), F32),
            buf((STEPS, 16, HEAD_DIM), F32),
            buf((STEPS, 16, HEAD_DIM), F32),
            buf((STEPS, 16, HEAD_DIM), F32),
            buf((STEPS, 16, 16 * HEAD_DIM), F32),
            buf((STEPS * 16, part), BF16),
            buf((8, 128, HEAD_DIM), BF16),
            buf((8, 128, HEAD_DIM), BF16),
            buf((NX, STEPS, 16, 128), F32),
            buf((NZ, BLOCK, WIDE), BF16),
            buf((CHUNKS, CLASSES, PER * SLAB, WIDE), BF16),
            buf((CHUNKS, peers, PER * SLAB, WIDE), BF16),
            buf((NX, part, 2 * HIDE), BF16),
            buf((NX * HIDE, part), BF16),
            buf((CHUNKS, PER * ROWS, 2 * HIDE), F32),
            buf((CHUNKS, NX, PER * ROWS, 2 * HIDE), BF16),
            buf((CHUNKS, NX, PER * ROWS, 2 * HIDE), BF16),
            buf((CHUNKS, NX, PER * ROWS, HIDE), BF16),
            buf((CHUNKS, peers, PER * SLAB, WIDE), BF16),
            buf((CHUNKS, peers, PER * SLAB, WIDE), BF16),
            buf((STRIDE, PACK, WIDE), F32),
            buf((CHUNKS, STRIDE, PACK, WIDE), BF16),
            buf((CHUNKS, STRIDE, PACK, WIDE), BF16),
            buf((STRIDE, PACK, WIDE), BF16),
            buf((STRIDE, PACK, WIDE), BF16),
            sem((6,)),
            sem((15,)),
            sem((2,)),
            sem((2, NX)),
            sem((2, NX, 2)),
            sem((2, 8)),
            sem((2, CHUNKS, peers)),
            sem((2, CHUNKS, NX)),
            sem((2, CHUNKS, NX)),
            sem((2, CHUNKS, peers)),
            sem((2, 5)),
            sem((2, STRIDE)),
        ],
        compiler_params=pltpu.CompilerParams(
            collective_id=0, has_side_effects=True, vmem_limit_bytes=63 * 1024 * 1024
        ),
    )(*operands)
    return attn, moe


def solution(mesh):
    return jax.shard_map(
        local,
        mesh=mesh,
        in_specs=(
            P(None, "dp", "rep"),
            P(None, "dp", "rep"),
            P(None, "dp", "rep"),
            P(),
            P(),
            P("dp", None, None, "rep"),
            P("dp", None),
            P("dp"),
            P("dp"),
            P("dp"),
            P(None, "dp", "rep"),
            P(),
            P(None, "dp", None),
            P(None, "dp", None),
            P("dp", None, "rep"),
            P("dp", None, "rep"),
            P("dp", None, "rep"),
        ),
        out_specs=(P(None, "dp", "rep"), P(None, "dp", "rep")),
        check_vma=False,
    )
```

time: 152 us -> 124 us (0.82)
  the two profiles are of different devices: /device:TPU:2 before, /device:TPU:1 now
where the time goes in v2:
time: 124 us
  Pallas kernels  120 us (97%)
  local copies, waits for them, and re-layouts  3.16 us (3%)
    pallas_call x1, Pallas kernels, local(): pl.pallas_call(kernel, out_shape=(jax.ShapeDtypeStruct((STEPS, REQ, 16 *...  120 us
    unnamed x2, local copies, waits for them, and re-layouts  3.16 us

profile of v2, /device:TPU:1, one launch (start us, length us, event | category | flops | bytes accessed | tf_op | source)
XLA Modules:
  0.0 124.1 jit_solution(14200930135370534153)
XLA Ops:
  0.6 120.3 %shard_map.185 = (bf16[3,12,2048]{2,1,0:T(8,128)(2,1)}, bf16[3,12,1024]{2,1,0:T(8,128)(2,1)}) custom-call(bf16[3,12,2048]{2,1,0:T(8,128)(2,1)} %q_hbm.1, bf16[3,12,128]{2,1,0:T(8,128)(2,1)} %k_hbm.1, bf16[3,12,128]{2,1,0:T(8,128)(2,1)} %v_hbm.1, f32[1,128]{1,0:T(1,128)} %bitcast.18, f32[1,128]{1,0:T(1,128)} %bitcast.19, bf16[48,128,128]{2,1,0:T(8,128)(2,1)} %bitcast.10, ...), custom_call_target="tpu_custom_call" | custom-call | tf_op jit(solution)/shard_map/pallas_call | solution.py:536
  120.9 1.6 %copy.22 = bf16[3,12,2048]{2,1,0:T(8,128)(2,1)} copy(bf16[3,12,2048]{2,1,0:T(8,128)(2,1)} %get-tuple-element.4) | data formatting | bytes 294912
  122.6 1.5 %copy.23 = bf16[3,12,1024]{2,1,0:T(8,128)(2,1)} copy(bf16[3,12,1024]{2,1,0:T(8,128)(2,1)} %get-tuple-element.5) | data formatting | bytes 147456

commit v3 on v2

--- a/solution.py
+++ b/solution.py
@@ -21,11 +21,12 @@
 WIDE = D // NX // LB
 STRIDE = 4
 CHUNKS = STRIDE
-PER = NZ // STRIDE // 2
+PER = NZ // STRIDE
 NEAR = (0, 1, -1, 2)
 FIRST, SECOND = 4, 8
-SLAB = LB * 2 * STEPS * 2
-ROWS = SLAB // LB * NY * NC
+PART = PER * STEPS * 2
+SLAB = LB * PART
+ROWS = PART * NY * NC
 CLASSES = 4
 SEL = CLASSES * SLAB
 HIDE = 128
@@ -34,22 +35,16 @@
 
 
 def tables():
-    peers, per = NY * NC, SLAB // LB
-    out = np.full((peers * SLAB + 8, 128), -1, np.float32)
+    out = np.full((SEL + 8, 128), -1, np.float32)
     row = 0
     for cls in range(CLASSES):
         for lb in range(LB):
-            for zz in range(2):
+            for j in range(PER):
                 for s in range(STEPS):
                     for slot in range(2):
-                        out[row, 4] = zz * PACK + s * LB * REQ + lb * REQ
-                        out[row, 5] = zz * 32 + cls * 8 + s * 2 + slot
+                        out[row, 0] = j * PACK + s * LB * REQ + lb * REQ
+                        out[row, 1] = j * 32 + cls * 8 + s * 2 + slot
                         row += 1
-    for lb in range(LB):
-        for q in range(peers):
-            for r in range(per):
-                a, b = (lb * peers + q) * per + r, q * SLAB + lb * per + r
-                out[a, 0], out[b, 1] = b, a
     for s in range(STEPS):
         for lb in range(LB):
             for i in range(REQ):
@@ -57,7 +52,7 @@
                 out[a, 2], out[b, 3] = b, a
     exponent = np.arange(HEAD_DIM // 2, dtype=np.float32) * np.float32(2.0 / HEAD_DIM)
     frequency = np.power(np.float32(THETA), -exponent).astype(np.float32)
-    out[peers * SLAB :] = np.concatenate([frequency, frequency])
+    out[SEL:] = np.concatenate([frequency, frequency])
     return out
 
 
@@ -80,8 +75,8 @@
     attn, moe,
     q_in, k_in, v_in, q_gain, k_gain, pool, page_table, lengths, out_pages, in_slots,
     hid, ln_gain, ids, logits, const,
-    spread, perm, perm_back, pack, unpack_rows, q_rows, k_rows, v_rows, cosines, sines, attn_rows,
-    natural, leave, arrive, stat, rows, chosen, taken, w_in, w_out,
+    spread, code_rows, shares, pack, unpack_rows, q_rows, k_rows, v_rows, cosines, sines, attn_rows,
+    natural, leave, arrive, stat, rows, near_out, chosen, taken, w_in, w_out,
     part_own, part_out, part_in, hidden, back_out, back_in, kept, home_out, home_in, last_out, last_in,
     local_sem, load_sem, page_sem, stat_sem, w_sem, row_sem, taken_sem,
     part_sem, hidden_sem, back_sem, home_sem, last_sem,
@@ -129,10 +124,11 @@
 
     def near_copies(n):
         if n < 3:
-            pieces = ((pl.ds(0, STRIDE), pl.ds(STRIDE * n, STRIDE), 3 + n, -NEAR[n]),)
-        else:
-            pieces = ((pl.ds(0, 2), pl.ds(12, 2), 6, -2), (pl.ds(2, 2), pl.ds(14, 2), 7, 2))
-        return [send(rows.at[a], rows.at[b], row_sem, (at,), along_z(by)) for a, b, at, by in pieces]
+            return [send(near_out.at[n], chosen.at[n], row_sem, (3 + n,), along_z(-NEAR[n]))]
+        return [
+            send(near_out.at[3, at], chosen.at[3, at], row_sem, (6 + m,), along_z(by))
+            for m, (at, by) in enumerate(((pl.ds(0, 2), -2), (pl.ds(2, 2), 2)))
+        ]
 
     def taken_copy(ch, by):
         other, device = peer(by)
@@ -260,9 +256,7 @@
     for copy in far_copies():
         copy.start()
 
-    spread[...] = one_hot(const[0:SEL, 5:6], 64)
-    perm[...] = one_hot(const[0 : NY * NC * SLAB, 0:1], NY * NC * SLAB)
-    perm_back[...] = one_hot(const[0 : NY * NC * SLAB, 1:2], NY * NC * SLAB)
+    spread[...] = one_hot(const[0:SEL, 1:2], PER * 32)
     unpack_rows[...] = one_hot(const[0 : LB * 48, 3:4], PACK)
     for name in ("len", "k", "v", "k_gain", "q_gain", "q", "table", "slots"):
         loads[name].wait()
@@ -276,7 +270,7 @@
     for i in range(REQ):
         start = jnp.where(request == i, lengths[i], start)
     sign = jnp.where(iota((16, 128), 1) < 64, -1.0, 1.0)
-    frequency = const[NY * NC * SLAB : NY * NC * SLAB + 1, :]
+    frequency = const[SEL : SEL + 1, :]
     for s in range(STEPS):
         angle = (start + s).astype(F32) * frequency
         cosines[s] = jnp.cos(angle)
@@ -286,23 +280,34 @@
         v_rows[s, 0:REQ, :] = v_in[s].astype(F32)
         q_rows[s, 0:REQ, :] = q_in[s].astype(F32)
 
-    def unpack(g):
-        pair = rows[pl.ds(2 * g, 2), PACK:BLOCK, :]
-        pair = jnp.concatenate([pair[zz, :, h * 128 : h * 128 + 128] for zz in range(2) for h in range(2)], axis=0)
+    def choose(n):
+        pair = rows[:, PACK:BLOCK, :]
+        pair = jnp.concatenate([pair[j, :, h * 128 : h * 128 + 128] for j in range(PER) for h in range(2)], axis=0)
         wide = dot(spread[...], pair)
         lane = iota((SEL, 128), 1)
-        code = jnp.sum(jnp.where(lane == z, wide, 0.0), axis=1, keepdims=True) + const[0:SEL, 4:5]
+        if n < 3:
+            there = (z + NZ - NEAR[n]) % NZ
+        else:
+            there = jnp.where(iota((SEL, 128), 0) < SEL // 2, (z + NZ - 2) % NZ, (z + 2) % NZ)
+        code = jnp.sum(jnp.where(lane == there, wide, 0.0), axis=1, keepdims=True) + const[0:SEL, 0:1]
         weight = jnp.sum(
-            jnp.where((lane == z + NZ) | (lane == z + 2 * NZ), wide, 0.0), axis=1, keepdims=True
+            jnp.where((lane == there + NZ) | (lane == there + 2 * NZ), wide, 0.0), axis=1, keepdims=True
         )
-        return code, weight
-
-    def choose(ch):
-        for u in range(PER):
-            g = ch * PER + u
-            code, _ = unpack(g)
-            picked = dot(one_hot(code, 2 * PACK), rows[pl.ds(2 * g, 2), 0:PACK, :].reshape(2 * PACK, WIDE)).astype(BF16)
-            chosen[ch, :, u * SLAB : (u + 1) * SLAB, :] = picked.reshape(CLASSES, SLAB, WIDE)
+        tokens = rows[:, 0:PACK, :].reshape(PER * PACK, WIDE)
+        picked = dot(one_hot(code, PER * PACK), tokens).astype(BF16).reshape(CLASSES, SLAB, WIDE)
+        if n:
+            near_out[n] = picked
+            for copy in near_copies(n):
+                copy.start()
+        else:
+            chosen[0] = picked
+            forward(0)
+        diagonal = iota((SEL, SEL), 0) == iota((SEL, SEL), 1)
+        code_row = jnp.sum(jnp.where(diagonal, code, 0.0), axis=0, keepdims=True)
+        code_rows[n] = jnp.broadcast_to(code_row, (8, SEL))
+        shares[n] = jnp.broadcast_to(weight, (SEL, 128))
+
+    def forward(ch):
         for by in range(1, 8):
             taken_copy(ch, by).start()
         taken[ch, q] = chosen[ch, y % 2 * NC + c]
@@ -351,10 +356,8 @@
 
     for copy in far_copies():
         copy.wait_recv()
-    for n in (1, 2, 3):
-        for copy in near_copies(n):
-            copy.start()
-    choose(0)
+    for n in (1, 2, 3, 0):
+        choose(n)
     page_copy().wait_recv()
     lax.fori_loop(0, FIRST, attend, 0)
 
@@ -365,7 +368,7 @@
                 for copy in near_copies(n):
                     copy.wait_recv()
 
-        choose(ch)
+        forward(ch)
         return carry
 
     lax.fori_loop(1, CHUNKS - 1, choose_next, 0)
@@ -379,14 +382,10 @@
     def first_matmul(ch):
         for by in range(1, 8):
             taken_copy(ch, by).wait_recv()
-        pieces = []
-        for u in range(PER):
-            slabs = taken[ch, :, u * SLAB : (u + 1) * SLAB, :].reshape(NY * NC * SLAB, WIDE)
-            block = dot(perm[...], slabs).astype(BF16)
-            pieces.append(
-                jnp.concatenate([block[lb * ROWS : (lb + 1) * ROWS] for lb in range(LB)], axis=1)
-            )
-        inputs = jnp.concatenate(pieces, axis=0)
+        slabs = taken[ch].astype(F32)
+        inputs = jnp.concatenate(
+            [slabs[:, lb * PART : (lb + 1) * PART, :].reshape(ROWS, WIDE) for lb in range(LB)], axis=1
+        ).astype(BF16)
         for by in (2, 1, 3):
             part_out[ch, by] = dot(inputs, w_in[(NX - by) % NX]).astype(BF16)
             part_copy(ch, by).start()
@@ -405,12 +404,10 @@
         for by in (1, 2, 3):
             hidden_copy(ch, by).wait_recv()
         units = jnp.concatenate([hidden[ch, by] for by in range(NX)], axis=1)
-        made = dot(units, w_out[...]).astype(BF16)
-        for u in range(PER):
-            part = made[u * ROWS : (u + 1) * ROWS]
-            stack = jnp.concatenate([part[:, lb * WIDE : (lb + 1) * WIDE] for lb in range(LB)], axis=0)
-            slabs = dot(perm_back[...], stack).astype(BF16)
-            back_out[ch, :, u * SLAB : (u + 1) * SLAB, :] = slabs.reshape(NY * NC, SLAB, WIDE)
+        made = dot(units, w_out[...]).reshape(NY * NC, PART, D // NX)
+        back_out[ch] = jnp.concatenate(
+            [made[:, :, lb * WIDE : (lb + 1) * WIDE] for lb in range(LB)], axis=1
+        ).astype(BF16)
         for by in range(1, 8):
             back_copy(ch, by).start()
         back_in[ch, q] = back_out[ch, q]
@@ -418,21 +415,12 @@
     def combine(ch):
         for by in range(1, 8):
             back_copy(ch, by).wait_recv()
-        for u in range(PER):
-            g = ch * PER + u
-            code, weight = unpack(g)
-            slabs = back_in[ch, :, u * SLAB : (u + 1) * SLAB, :].astype(F32)
-            both = (slabs[:CLASSES] + slabs[CLASSES:]).reshape(SEL, WIDE)
-            both = (both * weight).astype(BF16)
-            diagonal = iota((SEL, SEL), 0) == iota((SEL, SEL), 1)
-            code_row = jnp.sum(jnp.where(diagonal, code, 0.0), axis=0, keepdims=True)
-            at = iota((2 * PACK, SEL), 0).astype(F32)
-            sums = dot(jnp.where(at == code_row, 1.0, 0.0).astype(BF16), both)
-            home_out[ch, 2 * u : 2 * u + 2] = sums.astype(BF16).reshape(2, PACK, WIDE)
-
-            @pl.when(ch == 0)
-            def _(u=u, sums=sums):
-                kept[2 * u : 2 * u + 2] = sums.reshape(2, PACK, WIDE)
+        slabs = back_in[ch].astype(F32)
+        home_out[ch] = (slabs[:CLASSES] + slabs[CLASSES:]).astype(BF16)
+
+        @pl.when(ch == 0)
+        def _():
+            home_in[0] = home_out[0]
 
         for n in (1, 2, 3):
             @pl.when(ch == n)
@@ -466,16 +454,17 @@
     lax.fori_loop(0, CHUNKS + 3, experts, 0)
 
     lax.fori_loop(FIRST, SECOND, attend, 0)
-    for n in (1, 2, 3):
-        for copy in home_copies(n):
-            copy.wait_recv()
+    for n in (1, 2, 3, 0):
+        if n:
+            for copy in home_copies(n):
+                copy.wait_recv()
+        both = (home_in[n].astype(F32).reshape(SEL, WIDE) * shares[n, :, 0:1]).astype(BF16)
+        at = iota((PER * PACK, SEL), 0).astype(F32)
+        sums = dot(jnp.where(at == code_rows[n, 0:1, :], 1.0, 0.0).astype(BF16), both).reshape(PER, PACK, WIDE)
+        kept[...] = sums if n == 1 else kept[...] + sums
 
     def gathered(a):
-        at = (mine + a) % STRIDE
-        summed = kept[at]
-        for n in (1, 2, 3):
-            summed = summed + home_in[n, at].astype(F32)
-        return summed
+        return kept[(mine + a) % STRIDE]
 
     for a in (2, 1, 3):
         last_out[a] = gathered(a).astype(BF16)
@@ -542,9 +531,9 @@
         in_specs=[hbm] * len(operands),
         out_specs=(vmem, vmem),
         scratch_shapes=held + [
-            buf((SEL, 64), BF16),
-            buf((peers * SLAB, peers * SLAB), BF16),
-            buf((peers * SLAB, peers * SLAB), BF16),
+            buf((SEL, PER * 32), BF16),
+            buf((CHUNKS, 8, SEL), F32),
+            buf((CHUNKS, SEL, 128), F32),
             buf((PACK, LB * 48), BF16),
             buf((LB * 48, PACK), BF16),
             buf((STEPS, 16, 16 * HEAD_DIM), F32),
@@ -557,20 +546,21 @@
             buf((8, 128, HEAD_DIM), BF16),
             buf((8, 128, HEAD_DIM), BF16),
             buf((NX, STEPS, 16, 128), F32),
-            buf((NZ, BLOCK, WIDE), BF16),
-            buf((CHUNKS, CLASSES, PER * SLAB, WIDE), BF16),
-            buf((CHUNKS, peers, PER * SLAB, WIDE), BF16),
+            buf((STRIDE, BLOCK, WIDE), BF16),
+            buf((CHUNKS, CLASSES, SLAB, WIDE), BF16),
+            buf((CHUNKS, CLASSES, SLAB, WIDE), BF16),
+            buf((CHUNKS, peers, SLAB, WIDE), BF16),
             buf((NX, part, 2 * HIDE), BF16),
             buf((NX * HIDE, part), BF16),
-            buf((CHUNKS, PER * ROWS, 2 * HIDE), F32),
-            buf((CHUNKS, NX, PER * ROWS, 2 * HIDE), BF16),
-            buf((CHUNKS, NX, PER * ROWS, 2 * HIDE), BF16),
-            buf((CHUNKS, NX, PER * ROWS, HIDE), BF16),
-            buf((CHUNKS, peers, PER * SLAB, WIDE), BF16),
-            buf((CHUNKS, peers, PER * SLAB, WIDE), BF16),
+            buf((CHUNKS, ROWS, 2 * HIDE), F32),
+            buf((CHUNKS, NX, ROWS, 2 * HIDE), BF16),
+            buf((CHUNKS, NX, ROWS, 2 * HIDE), BF16),
+            buf((CHUNKS, NX, ROWS, HIDE), BF16),
+            buf((CHUNKS, peers, SLAB, WIDE), BF16),
+            buf((CHUNKS, peers, SLAB, WIDE), BF16),
             buf((STRIDE, PACK, WIDE), F32),
-            buf((CHUNKS, STRIDE, PACK, WIDE), BF16),
-            buf((CHUNKS, STRIDE, PACK, WIDE), BF16),
+            buf((CHUNKS, CLASSES, SLAB, WIDE), BF16),
+            buf((CHUNKS, CLASSES, SLAB, WIDE), BF16),
             buf((STRIDE, PACK, WIDE), BF16),
             buf((STRIDE, PACK, WIDE), BF16),
             sem((6,)),

time: 124 us -> 118 us (0.952)
  the two profiles are of different devices: /device:TPU:1 before, /device:TPU:17 now
where the time goes in v3:
time: 118 us; the launch traced here: 117 us
  Pallas kernels  114 us (97%)
  local copies, waits for them, and re-layouts  3.16 us (3%)
    pallas_call x1, Pallas kernels, local(): pl.pallas_call(kernel, out_shape=(jax.ShapeDtypeStruct((STEPS, REQ, 16 *...  114 us
    unnamed x2, local copies, waits for them, and re-layouts  3.16 us

profile of v3, /device:TPU:17, one launch (start us, length us, event | category | flops | bytes accessed | tf_op | source)
XLA Modules:
  0.0 117.4 jit_solution(8026574341111055942)
XLA Ops:
  0.6 113.6 %shard_map.185 = (bf16[3,12,2048]{2,1,0:T(8,128)(2,1)}, bf16[3,12,1024]{2,1,0:T(8,128)(2,1)}) custom-call(bf16[3,12,2048]{2,1,0:T(8,128)(2,1)} %q_hbm.1, bf16[3,12,128]{2,1,0:T(8,128)(2,1)} %k_hbm.1, bf16[3,12,128]{2,1,0:T(8,128)(2,1)} %v_hbm.1, f32[1,128]{1,0:T(1,128)} %bitcast.18, f32[1,128]{1,0:T(1,128)} %bitcast.19, bf16[48,128,128]{2,1,0:T(8,128)(2,1)} %bitcast.10, ...), custom_call_target="tpu_custom_call" | custom-call | tf_op jit(solution)/shard_map/pallas_call | solution.py:525
  114.3 1.6 %copy.22 = bf16[3,12,2048]{2,1,0:T(8,128)(2,1)} copy(bf16[3,12,2048]{2,1,0:T(8,128)(2,1)} %get-tuple-element.4) | data formatting | bytes 294912
  115.9 1.5 %copy.23 = bf16[3,12,1024]{2,1,0:T(8,128)(2,1)} copy(bf16[3,12,1024]{2,1,0:T(8,128)(2,1)} %get-tuple-element.5) | data formatting | bytes 147456
